TPU v7x, 128 devices: a whole 4x4x4 slice. The times are simulated.
128 devices in a mesh: seq: 16 (over y, z_lo, core), tp: 4 (over x), rep: 2 (over z_hi).
Axes of the slice: x: 4, y: 4, z: 4 (z_hi: 2, z_lo: 2; z = z_hi * 2 + z_lo), core: 2. Of those that a mesh axis runs over, the one named last changes fastest.
Arguments:
- tokens: bfloat16 [2, 12288, 3072], P('rep', 'seq'), may hold values from -6 to 6
- in_panels: bfloat16 [3072, 4, 4096], P(('seq', 'rep'), None, 'tp'), may hold values from -0.109375 to 0.109375
- out_panel: bfloat16 [4096, 3072], P('tp', ('seq', 'rep')), may hold values from -0.09375 to 0.09375
- decay_power: int32 [32], P('tp'), may hold values from 0 to 8
- boundary: int32 [2], P('rep'), may hold values from 1 to 12287
Outputs:
- layer_out: bfloat16 [2, 12288, 3072], P('rep', 'seq', 'tp')
All inputs are finite; a program needn't handle non-finite values.
Results may differ from a plain program's by a relative error of at most 0.019.
Values may be sent and summed in bfloat16 or wider, within the bound.
A program may use at most 128 MiB of HBM per device.

v0:
```python
import jax
import jax.numpy as jnp
from jax import lax
from jax.sharding import PartitionSpec as P

D = 3072
HDIM = 128


log_half = -0.6931471805599453
epsilon = 1e-06


def carried_in(value, axis, combine, identity):
    count, place = (lax.axis_size(axis), lax.axis_index(axis))
    everything = jax.tree.map(
        lambda part, kind: lax.all_gather(part.astype(kind), axis),
        value,
        (jnp.bfloat16, jnp.bfloat16),
    )
    start = jax.tree.map(
        lambda part, zero: jnp.broadcast_to(jnp.asarray(zero, part.dtype), part.shape),
        value,
        identity,
    )

    def turn(k, before):
        reached = k < place
        new = combine(
            before, jax.tree.map(lambda part, own: part[k].astype(own.dtype), everything, value)
        )
        return jax.tree.map(lambda a, b: jnp.where(reached, a, b), new, before)

    return lax.fori_loop(0, count, turn, start)


def attend_block(queries, key_rows, val_rows, state_in, log_rate, anchor, prompt_start):
    extent = queries.shape[0]
    positions = anchor + jnp.arange(extent, dtype=jnp.int32)
    newer_mask = positions >= prompt_start
    offsets = (positions[:, None] - positions[None, :]).astype(jnp.float32)
    allowed = (offsets >= 0.0) & (newer_mask[:, None] == newer_mask[None, :])
    weights = jnp.where(
        allowed[None], jnp.exp(log_rate[:, None, None] * jnp.maximum(offsets, 0.0)[None]), 0.0
    )
    scores = jnp.einsum("ihd,jhd->hij", queries, key_rows, preferred_element_type=jnp.float32)
    scores = (scores * weights).astype(jnp.bfloat16)
    within = jnp.einsum("hij,jhd->ihd", scores, val_rows, preferred_element_type=jnp.float32)
    use_prior = ((positions < prompt_start) | (anchor > prompt_start)).astype(jnp.float32)
    steps_in = (positions - anchor + 1).astype(jnp.float32)
    query_scale = jnp.exp(log_rate[None, :] * steps_in[:, None]) * use_prior[:, None]
    scaled = queries.astype(jnp.float32) * query_scale[:, :, None]
    across = jnp.einsum("ihd,hde->ihe", scaled, state_in, precision=lax.Precision.HIGHEST)
    final_pos = anchor + extent - 1
    kept_rows = (newer_mask == (final_pos >= prompt_start)).astype(jnp.float32)
    steps_out = (final_pos - positions).astype(jnp.float32)
    key_scale = jnp.exp(log_rate[None, :] * steps_out[:, None]) * kept_rows[:, None]
    decayed = (key_rows.astype(jnp.float32) * key_scale[:, :, None]).astype(jnp.bfloat16)
    local_state = jnp.einsum("jhd,jhe->hde", decayed, val_rows, preferred_element_type=jnp.float32)
    crossed = (anchor <= prompt_start) & (prompt_start <= final_pos)
    passing = jnp.exp(log_rate * extent) * jnp.where(crossed, 0.0, 1.0).astype(jnp.float32)
    return (within + across, local_state, passing)


def local(tokens, in_panels, out_panel, decay_power, boundary):
    slab_rows = tokens[0]
    extent = slab_rows.shape[0]
    seq_count = lax.axis_size("seq")
    own_index = lax.axis_index("seq")
    anchor = own_index * extent
    prompt_start = boundary[0]
    log_rate = log_half * jnp.exp2(decay_power.astype(jnp.float32)) / (extent * seq_count)
    head_count = decay_power.shape[0]
    width = in_panels.shape[2]
    full_in, full_out = (
        lax.all_gather(in_panels, ("seq", "rep"), axis=0, tiled=True),
        lax.all_gather(out_panel, ("seq", "rep"), axis=1, tiled=True),
    )
    projected = jnp.dot(
        slab_rows, full_in.reshape(D, 4 * width), preferred_element_type=jnp.float32
    )
    projected = projected.reshape(extent, 4, head_count, HDIM)
    queries = (jax.nn.silu(projected[:, 0]) * HDIM ** (-0.5)).astype(jnp.bfloat16)
    key_rows = jax.nn.silu(projected[:, 1]).astype(jnp.bfloat16)
    val_rows = projected[:, 2].astype(jnp.bfloat16)
    gate_rows = jax.nn.sigmoid(projected[:, 3])
    state = jnp.zeros((head_count, HDIM, HDIM), jnp.float32)
    passing_all = jnp.ones((head_count,), jnp.float32)
    block_out, local_state, passing = attend_block(
        queries, key_rows, val_rows, state, log_rate, anchor + 0, prompt_start
    )
    state = passing[:, None, None] * state + local_state
    passing_all = passing_all * passing
    attended = block_out

    def combine(earlier, later_part):
        return (
            earlier[0] * later_part[0],
            later_part[0][:, None, None] * earlier[1] + later_part[1],
        )

    identity = (
        jnp.ones((head_count,), jnp.float32),
        jnp.zeros((head_count, HDIM, HDIM), jnp.float32),
    )
    prior_rate, prior_state = carried_in((passing_all, state), "seq", combine, identity)
    positions = anchor + jnp.arange(extent, dtype=jnp.int32)
    use_prior = ((positions < prompt_start) | (anchor > prompt_start)).astype(jnp.float32)
    steps_in = jnp.arange(1, extent + 1, dtype=jnp.int32).astype(jnp.float32)
    query_scale = jnp.exp(log_rate[None, :] * steps_in[:, None]) * use_prior[:, None]
    scaled = queries.astype(jnp.float32) * query_scale[:, :, None]
    attended = attended + jnp.einsum(
        "ihd,hde->ihe", scaled, prior_state, precision=lax.Precision.HIGHEST
    )
    square = jnp.mean(attended * attended, axis=-1, keepdims=True)
    gated_rows = (
        (attended * lax.rsqrt(square + epsilon) * gate_rows)
        .astype(jnp.bfloat16)
        .reshape(extent, head_count * HDIM)
    )
    head_partial = jnp.dot(gated_rows, full_out, preferred_element_type=jnp.float32)
    summed = lax.psum_scatter(
        head_partial.astype(jnp.bfloat16), "tp", scatter_dimension=1, tiled=True
    )
    return summed[None]


def solution(mesh):
    return jax.shard_map(
        local,
        mesh=mesh,
        in_specs=(
            P("rep", "seq", None),
            P(("seq", "rep"), None, "tp"),
            P("tp", ("seq", "rep")),
            P("tp"),
            P("rep"),
        ),
        out_specs=P("rep", "seq", "tp"),
        check_vma=False,
    )
```

profile of v0, /device:TPU:32, one launch (start us, length us, event | category | flops | bytes accessed | tf_op | source)
XLA Modules:
  0.0 422.5 jit_solution(7838560214778880579)
XLA Ops:
  6.5 0.7 all-gather.6.cloned.1.call-update
  8.8 145.6 %all-gather.6.cloned.1.call-done = bf16[3072,4,1024]{2,1,0:T(4,128)(2,1)} async-done(((bf16[96,4,1024]{2,1,0:T(4,128)(2,1)}), bf16[3072,4,1024]{2,1,0:T(4,128)(2,1)}) %all-gather.6.cloned.1.call-update) | async-done | bytes 25165840 | tf_op jit(solution)/shard_map/all_gather | solution.py:76
  154.3 38.6 %copy.30 = bf16[3072,4,1024]{0,2,1:T(8,128)(2,1)} copy(bf16[3072,4,1024]{2,1,0:T(4,128)(2,1)} %all-gather.6.cloned.1.call-done) | data formatting | bytes 50331648 | tf_op jit(solution)/shard_map/reshape | solution.py:80
  192.9 24.5 %fusion.5 = f32[768,4,8,128]{0,3,2,1:T(8,128)S(1)} fusion(bf16[4,8,128,3072]{3,2,1,0:T(8,128)(2,1)} %bitcast.79, bf16[1,768,3072]{2,1,0:T(8,128)(2,1)} %param.7), kind=kOutput, calls=%fused_computation.8 | convolution fusion | flops 19327352832 | bytes 42467328 | tf_op jit(solution)/shard_map/dot_general | solution.py:79
  217.4 4.5 %copy-done = f32[768,4,8,128]{0,3,2,1:T(8,128)} copy-done((f32[768,4,8,128]{0,3,2,1:T(8,128)}, f32[768,4,8,128]{0,3,2,1:T(8,128)S(1)}, u32[]{:S(2)}) %copy-start) | copy-done | bytes 12582936
  222.0 1.7 fusion.23
  223.8 0.7 all-gather.8.cloned.1.call-update
  226.0 26.5 %all-reduce = bf16[128]{0:T(256)(128)(2,1)S(1)} all-reduce(bf16[128]{0:T(256)(128)(2,1)S(1)} %dynamic-update-slice), channel_id=2, replica_groups=mesh['seq'=16,'tp'=4,'rep'=2] {'seq'}, use_global_device_ids=true, to_apply=%add | all-reduce | flops 128 | bytes 512
  253.6 12.1 %fusion.1 = f32[8,128,768]{2,1,0:T(8,128)} fusion(f32[768,768]{1,0:T(8,128)S(1)} %convert_maximum_fusion, f32[8]{0:T(128)S(1)} %get-tuple-element.132, pred[768,768]{1,0:T(8,128)(4,1)S(1)} %fusion.16, f32[768,4,8,128]{0,3,2,1:T(8,128)} %copy-done), kind=kOutput, calls=%fused_computation.4 | convolution fusion | flops 2444230656 | bytes 15532064 | tf_op jit(solution)/shard_map/hij,jhd->ihd/dot_general | solution.py:48
  265.7 18.4 %while.14 = (s32[]{:T(128)}, f32[8,128,128]{2,1,0:T(8,128)S(1)}, s32[]{:T(128)}, bf16[16,8]{1,0:T(8,128)(2,1)S(1)}, bf16[16,8,128,128]{3,2,1,0:T(8,128)(2,1)}, /*index=5*/s32[]{:T(128)}, s32[]{:T(128)}) while((s32[]{:T(128)}, f32[8,128,128]{2,1,0:T(8,128)S(1)}, s32[]{:T(128)}, bf16[16,8]{1,0:T(8,128)(2,1)S(1)}, ...), condition=%wide.region_1.2_spmd.clone, body=%wide.region_0.1_spmd.clone.sunk | while | flops 655372 | bytes 1310913 | solution.py:34
  265.7 1.1 fusion.38
  266.9 1.1 fusion.38
  268.0 1.1 fusion.38
  269.1 1.1 fusion.38
  270.3 1.1 fusion.38
  271.4 1.1 fusion.38
  272.5 1.1 fusion.38
  273.7 1.1 fusion.38
  274.8 1.1 fusion.38
  276.0 1.1 fusion.38
  277.1 1.1 fusion.38
  278.3 1.1 fusion.38
  279.4 1.1 fusion.38
  280.5 1.1 fusion.38
  281.7 1.1 fusion.38
  282.8 1.1 fusion.38
  284.1 5.8 %fusion.13 = f32[8,128,768]{2,1,0:T(8,128)S(1)} fusion(f32[8,128,128]{2,1,0:T(8,128)S(1)} %get-tuple-element.99, f32[768,8]{0,1:T(8,128)S(1)} %get-tuple-element.130, f32[768,4,8,128]{0,3,2,1:T(8,128)} %copy-done), kind=kOutput, calls=%fused_computation.25 | convolution fusion | flops 1214251008 | bytes 6840320 | tf_op jit(solution)/shard_map/ihd,hde->ihe/dot_general | solution.py:112
  290.0 6.3 %fusion.12 = (f32[768,8]{0,1:T(8,128)S(1)}, f32[8,128,768]{2,1,0:T(8,128)S(1)}) fusion(f32[8,128,768]{2,1,0:T(8,128)S(1)} %fusion.13, f32[8,128,768]{2,1,0:T(8,128)S(1)} %copy-done.2, f32[768,8]{0,1:T(8,128)S(1)} %get-tuple-element.130, f32[768,4,8,128]{0,3,2,1:T(8,128)} %copy-done), kind=kOutput, calls=%fused_computation.21 | convolution fusion | flops 1217390592 | bytes 12632064 | tf_op jit(solution)/shard_map/ihd,hde->ihe/dot_general | solution.py:53
  296.3 2.8 fusion.15
  299.1 54.3 %all-gather.8.cloned.1.call-done = bf16[1024,3072]{0,1:T(8,128)(2,1)} async-done(((bf16[1024,96]{0,1:T(8,128)(2,1)}), bf16[1024,3072]{0,1:T(8,128)(2,1)}) %all-gather.8.cloned.1.call-update) | async-done | bytes 6291472 | tf_op jit(solution)/shard_map/all_gather | solution.py:77
  353.4 9.6 %convolution_convert_fusion = bf16[768,3072]{1,0:T(8,128)(2,1)} fusion(bf16[768,1024]{0,1:T(8,128)(2,1)S(1)} %bitcast.80, bf16[1024,3072]{0,1:T(8,128)(2,1)} %all-gather.8.cloned.1.call-done), kind=kOutput, calls=%fused_computation.7 | convolution fusion | flops 4834197504 | bytes 12582912 | tf_op jit(solution)/shard_map/dot_general | solution.py:121
  363.0 53.0 %reduce-scatter.2.cloned.1.call-done = bf16[768,768]{1,0:T(8,128)(2,1)} async-done(((bf16[768,3072]{1,0:T(8,128)(2,1)}), bf16[768,768]{1,0:T(8,128)(2,1)}) %reduce-scatter.2.cloned.1.call-update) | async-done | bytes 1179664 | tf_op jit(solution)/shard_map/reduce_scatter | solution.py:122
  (42 shorter events, 3.1 us)
Async XLA Ops:
  6.5 147.8 %all-gather.6.cloned.1.call-start = ((), (), s32[]{:S(2)}) async-start(), calls=%async_computation.1 | async-start | bytes 25952256 | tf_op jit(solution)/shard_map/all_gather | solution.py:76
  7.3 258.4 %all-gather.10.cloned.1.call-start = ((), (), s32[]{:S(2)}) async-start(), calls=%async_computation.4 | async-start | bytes 4456448 | tf_op jit(solution)/shard_map/all_gather | solution.py:17
  217.4 4.5 %copy-start = (f32[768,4,8,128]{0,3,2,1:T(8,128)}, f32[768,4,8,128]{0,3,2,1:T(8,128)S(1)}, u32[]{:S(2)}) copy-start(f32[768,4,8,128]{0,3,2,1:T(8,128)S(1)} %fusion.5) | copy-start | bytes 37748740
  222.0 2.6 copy-start.1
  223.7 129.6 %all-gather.8.cloned.1.call-start = ((), (), s32[]{:S(2)}) async-start(), calls=%async_computation.2 | async-start | bytes 6488064 | tf_op jit(solution)/shard_map/all_gather | solution.py:77
  224.5 191.5 %reduce-scatter.2.cloned.1.call-start = ((), (), s32[]{:S(2)}) async-start(), calls=%async_computation.3 | async-start | bytes 5898240 | tf_op jit(solution)/shard_map/reduce_scatter | solution.py:122
  284.1 5.9 %copy-start.2 = (f32[8,128,768]{2,1,0:T(8,128)S(1)}, f32[8,128,768]{2,1,0:T(8,128)}, u32[]{:S(2)}) copy-start(f32[8,128,768]{2,1,0:T(8,128)} %fusion.1) | copy-start | bytes 9437188
Sparse Core Ops, SparseCore 0:
  9.0 145.2 all-gather.5
  223.8 38.0 all-gather.9
  263.6 89.7 all-gather.7
  363.1 52.7 reduce-scatter.1
where the time goes:
time: 425 us; the launch traced here: 422 us
  waiting for transfers between devices  254 us (60%)
  matrix products  60 us (14%)
  local copies, waits for them, and re-layouts  44.1 us (10%)
  blocking collectives  26.5 us (6%)
  other arithmetic  22.3 us (5%)
  between operations  14.6 us (3%)
    all_gather x1, waiting for transfers between devices, local(): lax.all_gather(in_panels, ('seq', 'rep'), axis=0, tiled=True)  146 us
    all_gather x1, waiting for transfers between devices, local(): lax.all_gather(out_panel, ('seq', 'rep'), axis=1, tiled=True)  54.3 us
    reduce_scatter x1, waiting for transfers between devices, local(): lax.psum_scatter(head_partial.astype(jnp.bfloat16), 'tp', scatter_dimensi...  53 us
    reshape x1, local copies, waits for them, and re-layouts, local(): full_in.reshape(D, 4 * width)  38.6 us
    unnamed x1, blocking collectives  26.5 us
    dot_general x1, matrix products, local(): jnp.dot(slab_rows, full_in.reshape(D, 4 * width), preferred_element_type=...  24.5 us
    select_n x16, other arithmetic, turn(): return jax.tree.map(lambda a, b: jnp.where(reached, a, b), new, before)  17.5 us
    dot_general x1, matrix products, attend_block(): jnp.einsum('hij,jhd->ihd', scores, val_rows, preferred_element_type=jnp.f...  12.1 us
  transfers between devices with their start and end apart: 4, of which 3 were waited for; matrix products, arithmetic and copies ran while one was open for 11% of the time, Pallas kernels for 0%

commit v1 on v0

v1 whole, which is shorter than its diff:
```python
import jax
import jax.numpy as jnp
from jax import lax
from jax.sharding import PartitionSpec as P

D = 3072
HDIM = 128


log_half = -0.6931471805599453
epsilon = 1e-06


def attend_block(queries, key_rows, val_rows, log_rate, anchor, prompt_start):
    extent = queries.shape[0]
    positions = anchor + jnp.arange(extent, dtype=jnp.int32)
    newer_mask = positions >= prompt_start
    offsets = (positions[:, None] - positions[None, :]).astype(jnp.float32)
    allowed = (offsets >= 0.0) & (newer_mask[:, None] == newer_mask[None, :])
    weights = jnp.where(
        allowed[None], jnp.exp(log_rate[:, None, None] * jnp.maximum(offsets, 0.0)[None]), 0.0
    )
    scores = jnp.einsum("ihd,jhd->hij", queries, key_rows, preferred_element_type=jnp.float32)
    scores = (scores * weights).astype(jnp.bfloat16)
    within = jnp.einsum("hij,jhd->ihd", scores, val_rows, preferred_element_type=jnp.float32)
    final_pos = anchor + extent - 1
    kept_rows = (newer_mask == (final_pos >= prompt_start)).astype(jnp.float32)
    steps_out = (final_pos - positions).astype(jnp.float32)
    key_scale = jnp.exp(log_rate[None, :] * steps_out[:, None]) * kept_rows[:, None]
    decayed = (key_rows.astype(jnp.float32) * key_scale[:, :, None]).astype(jnp.bfloat16)
    local_state = jnp.einsum("jhd,jhe->hde", decayed, val_rows, preferred_element_type=jnp.float32)
    return within, local_state


def local(tokens, in_panels, out_panel, decay_power, boundary):
    slab_rows = tokens[0]
    extent = slab_rows.shape[0]
    seq_count = lax.axis_size("seq")
    own_index = lax.axis_index("seq")
    anchor = own_index * extent
    prompt_start = boundary[0]
    log_rate = log_half * jnp.exp2(decay_power.astype(jnp.float32)) / (extent * seq_count)
    head_count = decay_power.shape[0]
    width = in_panels.shape[2]
    flat_in = lax.optimization_barrier(in_panels.reshape(in_panels.shape[0], 4 * width))
    full_in = lax.all_gather(flat_in, ("seq", "rep"), axis=0, tiled=True)
    full_out = lax.all_gather(out_panel.T, ("seq", "rep"), axis=0, tiled=True)
    projected = jnp.dot(slab_rows, full_in, preferred_element_type=jnp.float32)
    projected = lax.optimization_barrier(projected)
    projected = projected.reshape(extent, 4, head_count, HDIM)
    queries = (jax.nn.silu(projected[:, 0]) * HDIM ** (-0.5)).astype(jnp.bfloat16)
    key_rows = jax.nn.silu(projected[:, 1]).astype(jnp.bfloat16)
    val_rows = projected[:, 2].astype(jnp.bfloat16)
    gate_rows = jax.nn.sigmoid(projected[:, 3])
    within, local_state = attend_block(
        queries, key_rows, val_rows, log_rate, anchor, prompt_start
    )
    states = lax.all_gather(local_state.astype(jnp.bfloat16), "seq")
    owners = jnp.arange(seq_count, dtype=jnp.int32)
    between = (own_index - 1 - owners).astype(jnp.float32)
    crossing = prompt_start // extent
    reaches = (owners < own_index) & ~((owners < crossing) & (crossing < own_index))
    carry = jnp.where(
        reaches[:, None],
        jnp.exp(log_rate[None, :] * extent * jnp.maximum(between, 0.0)[:, None]),
        0.0,
    )
    prior_state = jnp.sum(carry[:, :, None, None] * states.astype(jnp.float32), axis=0)
    attended = within
    positions = anchor + jnp.arange(extent, dtype=jnp.int32)
    use_prior = ((positions < prompt_start) | (anchor > prompt_start)).astype(jnp.float32)
    steps_in = jnp.arange(1, extent + 1, dtype=jnp.int32).astype(jnp.float32)
    query_scale = jnp.exp(log_rate[None, :] * steps_in[:, None]) * use_prior[:, None]
    scaled = queries.astype(jnp.float32) * query_scale[:, :, None]
    attended = attended + jnp.einsum(
        "ihd,hde->ihe", scaled, prior_state, precision=lax.Precision.HIGHEST
    )
    square = jnp.mean(attended * attended, axis=-1, keepdims=True)
    gated_rows = (
        (attended * lax.rsqrt(square + epsilon) * gate_rows)
        .astype(jnp.bfloat16)
        .reshape(extent, head_count * HDIM)
    )
    head_partial = lax.dot_general(
        gated_rows, full_out, (((1,), (1,)), ((), ())), preferred_element_type=jnp.float32
    )
    summed = lax.psum_scatter(
        head_partial.astype(jnp.bfloat16), "tp", scatter_dimension=1, tiled=True
    )
    return summed[None]


def solution(mesh):
    return jax.shard_map(
        local,
        mesh=mesh,
        in_specs=(
            P("rep", "seq", None),
            P(("seq", "rep"), None, "tp"),
            P("tp", ("seq", "rep")),
            P("tp"),
            P("rep"),
        ),
        out_specs=P("rep", "seq", "tp"),
        check_vma=False,
    )
```

time: 425 us -> 411 us (0.967)
  waiting for transfers between devices: 254 us -> 295 us
  blocking collectives: 26.5 us -> 0 us
  local copies, waits for them, and re-layouts: 44.1 us -> 29.8 us
  other arithmetic: 22.3 us -> 8.14 us
    all_gather x3, waiting for transfers between devices: 200 us -> 241 us  [the longest x1 144 us: local(): full_in = lax.all_gather(flat_in, ('seq', 'rep'), axis=0, tiled=True)]
    reshape x1 -> x0, local copies, waits for them, and re-layouts: 38.6 us -> none  [local(): full_in.reshape(D, 4 * width)]
    unnamed x1 -> x0, blocking collectives: 26.5 us -> none
    select_n x16 -> x1, other arithmetic: 17.5 us -> 0.08 us  [local(): jnp.where(reaches[:, None], jnp.exp(log_rate[None, :] * extent * jnp.maxi...]
    unnamed x9 -> x8, local copies, waits for them, and re-layouts: 5.38 us -> 19.6 us
    slice x0 -> x2, local copies, waits for them, and re-layouts: none -> 10.2 us  [the longest x1 6.98 us: local(): gate_rows = jax.nn.sigmoid(projected[:, 3])]
    dot_general x3 -> x2, matrix products: 40.4 us -> 35.7 us  [the longest x1 26 us: local(): projected = jnp.dot(slab_rows, full_in, preferred_element_type=jnp.float32)]
  transfers between devices with their start and end apart: 4 -> 4, of which waited for: 3 -> 4; matrix products, arithmetic and copies ran while one was open for 11% -> 8% of each run, Pallas kernels for 0% -> 0%
where the time goes in v1:
time: 411 us; the launch traced here: 409 us
  waiting for transfers between devices  295 us (72%)
  matrix products  62.2 us (15%)
  local copies, waits for them, and re-layouts  29.8 us (7%)
  between operations  13.9 us (3%)
  other arithmetic  8.14 us (2%)
    all_gather x1, waiting for transfers between devices, local(): full_in = lax.all_gather(flat_in, ('seq', 'rep'), axis=0, tiled=True)  144 us
    all_gather x1, waiting for transfers between devices, local(): full_out = lax.all_gather(out_panel.T, ('seq', 'rep'), axis=0, tiled=True)  79.5 us
    reduce_scatter x1, waiting for transfers between devices, local(): lax.psum_scatter(head_partial.astype(jnp.bfloat16), 'tp', scatter_dimensi...  52.9 us
    dot_general x1, matrix products, local(): projected = jnp.dot(slab_rows, full_in, preferred_element_type=jnp.float32)  26 us
    unnamed x8, local copies, waits for them, and re-layouts  19.6 us
    all_gather x1, waiting for transfers between devices, local(): states = lax.all_gather(local_state.astype(jnp.bfloat16), 'seq')  17.9 us
    dot_general x1, matrix products, attend_block(): jnp.einsum('hij,jhd->ihd', scores, val_rows, preferred_element_type=jnp.f...  13.6 us
    dot_general x1, matrix products, local(): lax.dot_general(gated_rows, full_out, (((1,), (1,)), ((), ())), preferred...  9.71 us
  transfers between devices with their start and end apart: 4, of which 4 were waited for; matrix products, arithmetic and copies ran while one was open for 8% of the time, Pallas kernels for 0%

profile of v1, /device:TPU:32, one launch (start us, length us, event | category | flops | bytes accessed | tf_op | source)
XLA Modules:
  0.0 409.2 jit_solution(10307200429481321164)
XLA Ops:
  6.5 0.0 all-gather.5.cloned.1.call-start
  6.5 2.3 copy.26
  8.8 0.0 all-gather.5.cloned.1.call-update
  8.8 0.0 all-gather.9.cloned.1.call-start
  9.6 0.7 broadcast_multiply_fusion
  10.3 0.1 exponential_multiply_fusion
  10.4 144.0 %all-gather.5.cloned.1.call-done = bf16[3072,4096]{1,0:T(8,128)(2,1)} async-done(((bf16[96,4096]{1,0:T(8,128)(2,1)}), bf16[3072,4096]{1,0:T(8,128)(2,1)}) %all-gather.5.cloned.1.call-update) | async-done | bytes 25165840 | tf_op jit(solution)/shard_map/all_gather | solution.py:46
  154.4 26.0 %fusion.5 = f32[768,4096]{1,0:T(8,128)} fusion(bf16[3072,4096]{1,0:T(8,128)(2,1)} %all-gather.5.cloned.1.call-done, bf16[1,768,3072]{2,1,0:T(8,128)(2,1)} %param.5), kind=kOutput, calls=%fused_computation.7 | convolution fusion | flops 19327352832 | bytes 42467328 | tf_op jit(solution)/shard_map/dot_general | solution.py:48
  180.4 12.0 %copy.27 = f32[96,8,32,128]{3,2,1,0:T(8,128)} copy(f32[96,8,32,128]{3,1,2,0:T(8,128)} %bitcast.65) | data formatting | bytes 25165824
  192.4 7.0 %fusion.31 = (f32[768,1,8,128]{3,2,1,0:T(8,128)S(1)}, f32[768,1,8,128]{3,2,1,0:T(8,128)}, f32[768,1,8,128]{3,2,1,0:T(8,128)}) fusion(f32[768,4,8,128]{3,2,1,0:T(8,128)} %bitcast.63), kind=kLoop, calls=%fused_computation.52 | loop fusion | bytes 18874368 | tf_op jit(solution)/shard_map/slice | solution.py:54
  199.4 3.2 slice.17
  202.6 2.9 copy.24
  205.5 4.9 %fusion.21 = bf16[8,128,128]{2,1,0:T(8,128)(2,1)} fusion(f32[768,8]{0,1:T(8,128)S(1)} %get-tuple-element.9, bf16[768,1,8,128]{0,3,2,1:T(8,128)(2,1)} %copy.24, f32[768,1,8,128]{3,2,1,0:T(8,128)} %get-tuple-element.7), kind=kOutput, calls=%fused_computation.31 | convolution fusion | flops 207749120 | bytes 5005312 | tf_op jit(solution)/shard_map/jhd,jhe->hde/dot_general | solution.py:31
  210.4 0.0 all-gather.9.cloned.1.call-update
  210.4 0.0 all-gather.7.cloned.1.call-start
  210.5 0.7 all-gather.7.cloned.1.call-update
  211.2 0.0 reduce-scatter.2.cloned.1.call-start
  211.3 0.1 exponential_select_fusion
  211.3 1.5 fusion.12
  212.8 1.8 convert_maximum_fusion
  214.6 2.5 copy.25
  217.1 13.6 %fusion = f32[8,128,768]{2,1,0:T(8,128)} fusion(f32[768,768]{1,0:T(8,128)} %convert_maximum_fusion, f32[8]{0:T(128)S(1)} %get-tuple-element.11, pred[768,768]{1,0:T(8,128)(4,1)} %fusion.12, bf16[768,1,8,128]{0,3,2,1:T(8,128)(2,1)} %copy.24, f32[768,1,8,128]{3,2,1,0:T(8,128)} %get-tuple-element.7, f32[768,1,8,128]{3,2,1,0:T(8,128)} %get-tuple-element.6), kind=kOutput, calls=%fused_computation.1 | convolution fusion | flops 2443444224 | bytes 13959200 | tf_op jit(solution)/shard_map/hij,jhd->ihd/dot_general | solution.py:25
  230.6 17.9 %all-gather.9.cloned.1.call-done = bf16[128,128,128]{2,1,0:T(8,128)(2,1)} async-done(((bf16[8,128,128]{2,1,0:T(8,128)(2,1)}), bf16[128,128,128]{2,1,0:T(8,128)(2,1)}) %all-gather.9.cloned.1.call-update) | async-done | bytes 4194320 | tf_op jit(solution)/shard_map/all_gather | solution.py:58
  248.5 3.1 fusion.2
  251.6 0.0 copy-done.1
  251.7 8.0 %fusion.8 = (f32[768,8]{0,1:T(8,128)S(1)}, f32[8,128,768]{2,1,0:T(8,128)S(1)}) fusion(f32[8,128,768]{2,1,0:T(8,128)} %fusion, f32[8,128,128]{2,1,0:T(8,128)S(1)} %fusion.2, f32[768,8]{0,1:T(8,128)S(1)} %get-tuple-element.8, f32[768,1,8,128]{3,2,1,0:T(8,128)S(1)} %copy-done.1), kind=kOutput, calls=%fused_computation.15 | convolution fusion | flops 1216604160 | bytes 10010624 | tf_op jit(solution)/shard_map/ihd,hde->ihe/dot_general | solution.py:75
  259.7 0.0 copy-done
  259.7 0.9 fusion.7
  260.6 79.5 %all-gather.7.cloned.1.call-done = bf16[3072,1024]{1,0:T(8,128)(2,1)} async-done(((bf16[96,1024]{1,0:T(8,128)(2,1)}), bf16[3072,1024]{1,0:T(8,128)(2,1)}) %all-gather.7.cloned.1.call-update) | async-done | bytes 6291472 | tf_op jit(solution)/shard_map/all_gather | solution.py:47
  340.0 9.7 %convolution_convert_fusion = bf16[768,3072]{1,0:T(8,128)(2,1)} fusion(bf16[768,1024]{0,1:T(8,128)(2,1)S(1)} %bitcast.68, bf16[3072,1024]{1,0:T(8,128)(2,1)} %all-gather.7.cloned.1.call-done), kind=kOutput, calls=%fused_computation.6 | convolution fusion | flops 4834197504 | bytes 12582912 | tf_op jit(solution)/shard_map/dot_general | solution.py:84
  349.7 0.0 reduce-scatter.2.cloned.1.call-update
  349.8 52.9 %reduce-scatter.2.cloned.1.call-done = bf16[768,768]{1,0:T(8,128)(2,1)} async-done(((bf16[768,3072]{1,0:T(8,128)(2,1)}), bf16[768,768]{1,0:T(8,128)(2,1)}) %reduce-scatter.2.cloned.1.call-update) | async-done | bytes 1179664 | tf_op jit(solution)/shard_map/reduce_scatter | solution.py:87
  (9 shorter events, 0.1 us)
Async XLA Ops:
  6.5 147.8 %all-gather.5.cloned.1.call-start = ((), (), s32[]{:S(2)}) async-start(), calls=%async_computation.1 | async-start | bytes 25952256 | tf_op jit(solution)/shard_map/all_gather | solution.py:46
  8.8 239.7 %all-gather.9.cloned.1.call-start = ((), (), s32[]{:S(2)}) async-start(), calls=%async_computation.4 | async-start | bytes 4456448 | tf_op jit(solution)/shard_map/all_gather | solution.py:58
  210.4 129.6 %all-gather.7.cloned.1.call-start = ((), (), s32[]{:S(2)}) async-start(), calls=%async_computation.2 | async-start | bytes 6488064 | tf_op jit(solution)/shard_map/all_gather | solution.py:47
  211.2 191.5 %reduce-scatter.2.cloned.1.call-start = ((), (), s32[]{:S(2)}) async-start(), calls=%async_computation.3 | async-start | bytes 5898240 | tf_op jit(solution)/shard_map/reduce_scatter | solution.py:87
  230.6 21.0 %copy-start.1 = (f32[768,1,8,128]{3,2,1,0:T(8,128)S(1)}, f32[768,1,8,128]{3,2,1,0:T(8,128)}, u32[]{:S(2)}) copy-start(f32[768,1,8,128]{3,2,1,0:T(8,128)} %get-tuple-element.6) | copy-start | bytes 9437188
  251.6 8.0 %copy-start = (f32[768,1,8,128]{0,3,2,1:T(8,128)S(1)}, f32[768,1,8,128]{0,3,2,1:T(8,128)}, u32[]{:S(2)}) copy-start(f32[768,1,8,128]{0,3,2,1:T(8,128)} %copy.25) | copy-start | bytes 9437188
Sparse Core Ops, SparseCore 0:
  9.0 145.2 all-gather.4
  210.5 37.9 all-gather.8
  250.2 89.7 all-gather.6
  349.9 52.7 reduce-scatter.1

commit v2 on v1

v2 whole, which is shorter than its diff:
```python
import functools

import jax
import jax.numpy as jnp
from jax import lax
from jax.experimental import pallas as pl
from jax.experimental.pallas import tpu as pltpu
from jax.sharding import PartitionSpec as P

HDIM = 128
MESH = pl.DeviceIdType.MESH
log_half = -0.6931471805599453
epsilon = 1e-06
F32 = jnp.float32
BF16 = jnp.bfloat16


def nt_dot(a, b):
    return lax.dot_general(a, b, (((1,), (1,)), ((), ())), preferred_element_type=F32)


def tn_dot(a, b):
    return lax.dot_general(a, b, (((0,), (0,)), ((), ())), preferred_element_type=F32)


def kernel(
    heads, rates, coef, place, tok, wsh, osh, out,
    G, tokv, gall, qbuf, wbuf, gbuf, pbuf, lbuf, tbuf, acc,
    loc, s1, r1, s2, r2, ssib, rsib, sa, ra, sl, rl, st, rt, sx, rx,
):
    extent = tok.shape[0]
    rows = wsh.shape[2]
    half = rows // 2
    steps = heads + 2
    pieces = steps // 2
    rem, div = lax.rem, lax.div
    s, x, zhi = lax.axis_index("seq"), lax.axis_index("tp"), lax.axis_index("rep")
    y, g, zlo, c = div(s, 4), rem(s, 4), rem(div(s, 2), 2), rem(s, 2)
    z = zhi * 2 + zlo

    def around(k, d):
        return rem(k + d, 4)

    def at_y(k):
        return {"seq": k * 4 + g}

    def at_z(k):
        return {"seq": y * 4 + rem(k, 2) * 2 + c, "rep": div(k, 2)}

    def at_g(k):
        return {"seq": y * 4 + k}

    def at_x(k):
        return {"tp": k}

    sibling = {"seq": y * 4 + zlo * 2 + 1 - c}

    def dest(q):
        return {"tp": y, "seq": q * 4 + g}

    def source(k):
        return {"tp": k, "seq": x * 4 + g}

    corner = x == y

    barrier = pltpu.get_barrier_semaphore()

    def greet(device):
        pl.semaphore_signal(barrier, inc=1, device_id=device, device_id_type=MESH)

    own_copies = [
        pltpu.make_async_copy(tok, tokv, loc.at[0]),
        pltpu.make_async_copy(wsh, G.at[pl.ds(0, heads), :, y, zlo, c, zhi], loc.at[1]),
    ]
    own_copies[1].start()
    for d in (1, 2, 3):
        greet(at_y(around(y, d)))
        greet(at_g(around(g, d)))
    for d in (1, 3):
        greet(at_z(around(z, d)))
        greet(at_x(around(x, d)))
    for k in range(4):
        @pl.when(jnp.logical_not(corner & (y == k)))
        def _():
            greet(dest(k))
        @pl.when(jnp.logical_not(corner & (x == k)))
        def _():
            greet(source(k))
    pl.semaphore_wait(barrier, 10 + jnp.where(corner, 6, 8))

    def send(src, dst, ss, rs, device):
        pltpu.make_async_remote_copy(
            src_ref=src, dst_ref=dst, send_sem=ss, recv_sem=rs, device_id=device, device_id_type=MESH
        ).start()

    def got(ref, ss, rs):
        pltpu.make_async_remote_copy(
            src_ref=ref, dst_ref=ref, send_sem=ss, recv_sem=rs, device_id=sibling, device_id_type=MESH
        ).wait_recv()

    def sent(ref, ss, rs):
        pltpu.make_async_remote_copy(
            src_ref=ref, dst_ref=ref, send_sem=ss, recv_sem=rs, device_id=sibling, device_id_type=MESH
        ).wait_send()

    first_ring = ((y, at_y), (z, at_z))
    second_ring = ((z, at_z), (y, at_y))

    def unit1(m, a, k, lo=0, n=rows):
        if a == 0:
            return G.at[pl.ds(2 * m, 2), 0, k, zlo, c, zhi, pl.ds(lo, n)]
        return G.at[pl.ds(2 * m, 2), 1, y, rem(k, 2), c, div(k, 2), pl.ds(lo, n)]

    def unit2(t, a, k):
        if a == 0:
            return G.at[t, 0, :, rem(k, 2), c, div(k, 2)]
        return G.at[t, 1, k, :, c]

    def half2(t, a, k, part):
        if a == 0:
            return G.at[t, 0, pl.ds(2 * part, 2), rem(k, 2), c, div(k, 2)]
        return G.at[t, 1, k, pl.ds(part, 1), c]

    def first_send(m):
        for a in (0, 1):
            k, at = first_ring[a]
            own = unit1(m, a, k)
            for d, step in ((0, 1), (1, 3)):
                send(own, own, s1.at[m, a, d], r1.at[m, a, d], at(around(k, step)))

    def first_pass(m):
        for a in (0, 1):
            k, at = first_ring[a]
            for d, step in ((0, 1), (1, 3)):
                origin = around(k, 4 - step)
                got(unit1(m, a, origin), s1.at[m, a, d], r1.at[m, a, d])
                part = unit1(m, a, origin, d * half, half)
                send(part, part, s1.at[m, a, 2 + d], r1.at[m, a, 2 + d], at(around(k, step)))

    def first_end(m):
        for a in (0, 1):
            k, _ = first_ring[a]
            for d in (0, 1):
                part = unit1(m, a, around(k, 2), d * half, half)
                got(part, s1.at[m, a, 2 + d], r1.at[m, a, 2 + d])

    def second_send(t):
        for a in (1, 0):
            k, at = second_ring[a]
            own = unit2(t, a, k)
            for d, step in ((0, 1), (1, 3)):
                send(own, own, s2.at[t, a, d], r2.at[t, a, d], at(around(k, step)))

    def second_pass(t):
        for a in (1, 0):
            k, at = second_ring[a]
            for d, step in ((0, 1), (1, 3)):
                origin = around(k, 4 - step)
                got(unit2(t, a, origin), s2.at[t, a, d], r2.at[t, a, d])
                part = half2(t, a, origin, d)
                send(part, part, s2.at[t, a, 2 + d], r2.at[t, a, 2 + d], at(around(k, step)))

    def second_end(t):
        for a in (1, 0):
            k, _ = second_ring[a]
            for d in (0, 1):
                got(half2(t, a, around(k, 2), d), s2.at[t, a, 2 + d], r2.at[t, a, 2 + d])

    def share(t):
        mine = G.at[t, :, :, :, c]
        send(mine, mine, ssib.at[t], rsib.at[t], sibling)

    def shared(t):
        got(G.at[t, :, :, :, 1 - c], ssib.at[t], rsib.at[t])

    def out_unit(k, q):
        return G.at[heads + div(k, 2), rem(k, 2), q, zlo, c, zhi]

    own_copies[1].wait()
    first_send(0)
    first_send(1)
    for q in range(4):
        width = osh.shape[1] // 4
        columns = osh.at[:, pl.ds(q * width, width)]
        is_own = corner & (y == q)
        @pl.when(is_own)
        def _():
            pltpu.make_async_copy(columns, out_unit(x, q), loc.at[2]).start()
        @pl.when(jnp.logical_not(is_own))
        def _():
            send(columns, out_unit(x, q), sa.at[q], ra.at[x], dest(q))
    own_copies[0].start()
    first_pass(0)
    first_send(2)
    first_pass(1)
    first_end(0)
    second_send(0)
    second_send(1)
    first_pass(2)
    first_end(1)
    second_send(2)
    first_send(3)
    own_copies[0].wait()
    second_pass(0)
    for k in range(4):
        is_own = corner & (x == k)
        @pl.when(is_own)
        def _():
            pltpu.make_async_copy(osh.at[:, pl.ds(0, osh.shape[1] // 4)], out_unit(k, y), loc.at[2]).wait()
        @pl.when(jnp.logical_not(is_own))
        def _():
            got(out_unit(k, y), sa.at[k], ra.at[k])
    acc[...] = jnp.zeros_like(acc)

    edge = place[0]
    down = lax.broadcasted_iota(jnp.int32, (extent, HDIM), 0)
    BR = 256

    def project(h):
        slot = rem(h, 4)
        rate = rates[h]
        panel = G[h, 0].reshape(-1, 2 * HDIM)
        u = jnp.dot(tokv[...], panel, preferred_element_type=F32)
        down_f = down.astype(F32)
        grow = jnp.exp(rate * down_f)
        shrink = jnp.exp(-rate * down_f)
        uq, uk = u[:, :HDIM], u[:, HDIM:]
        q = ((uq / (1.0 + jnp.exp(-uq))) * (HDIM ** -0.5) * grow).astype(BF16)
        kf = (uk / (1.0 + jnp.exp(-uk))) * shrink
        k = kf.astype(BF16)
        kept = jnp.where((down >= edge) | (edge >= extent), kf, 0.0).astype(BF16)
        panel = G[h, 1].reshape(-1, 2 * HDIM)
        u = jnp.dot(tokv[...], panel, preferred_element_type=F32)
        v = u[:, :HDIM].astype(BF16)
        gbuf[slot] = 1.0 / (1.0 + jnp.exp(-u[:, HDIM:]))
        qbuf[slot] = q
        lbuf[h, g] = (tn_dot(kept, v) * coef[h, 13]).astype(BF16)
        for d in (1, 2, 3):
            own = lbuf.at[h, g]
            send(own, own, sl.at[h, d - 1], rl.at[h, d - 1], at_g(around(g, d)))
        for lo in range(0, extent, BR):
            hi = lo + BR
            scores = nt_dot(q[lo:hi], k[:hi])
            i = lax.broadcasted_iota(jnp.int32, (BR, hi), 0) + lo
            j = lax.broadcasted_iota(jnp.int32, (BR, hi), 1)
            keep = (j <= i) & (j >= jnp.where(i >= edge, edge, 0))
            scores = jnp.where(keep, scores, 0.0).astype(BF16)
            wbuf[slot, pl.ds(lo, BR)] = jnp.dot(scores, v[:hi], preferred_element_type=F32)

    def gather_states(h):
        for d in (1, 2, 3):
            got(lbuf.at[h, around(g, 4 - d)], sl.at[h, d - 1], rl.at[h, d - 1])
        total = jnp.zeros((HDIM, HDIM), F32)
        before = jnp.zeros((HDIM, HDIM), F32)
        for k in range(4):
            part = lbuf[h, k].astype(F32)
            total += coef[h, k] * part
            before += coef[h, 4 + k] * part
        pbuf[rem(h, 4)] = before
        tbuf[h, y] = total.astype(BF16)
        for d in (1, 2, 3):
            own = tbuf.at[h, y]
            send(own, own, st.at[h, d - 1], rt.at[h, d - 1], at_y(around(y, d)))

    def finish(h):
        slot = rem(h, 4)
        for d in (1, 2, 3):
            got(tbuf.at[h, around(y, 4 - d)], st.at[h, d - 1], rt.at[h, d - 1])
        state = pbuf[slot]
        for k in range(4):
            state += coef[h, 8 + k] * tbuf[h, k].astype(F32)
        use = jnp.where((down < edge) | (edge < 0), coef[h, 12], 0.0)
        across = jnp.dot(qbuf[slot], state.astype(BF16), preferred_element_type=F32)
        attended = wbuf[slot] + across * use
        square = jnp.mean(attended * attended, axis=-1, keepdims=True)
        gall[x, h] = (attended * lax.rsqrt(square + epsilon) * gbuf[slot]).astype(BF16)
        own = gall.at[x, h]
        for d, step in ((0, 1), (1, 3)):
            send(own, own, sx.at[h, d], rx.at[h, d], at_x(around(x, step)))

    def half_rows(k, h, d):
        return gall.at[k, h, pl.ds(d * (extent // 2), extent // 2)]

    def pass_gated(h):
        for d, step in ((0, 1), (1, 3)):
            origin = around(x, 4 - step)
            got(gall.at[origin, h], sx.at[h, d], rx.at[h, d])
            part = half_rows(origin, h, d)
            send(part, part, sx.at[h, 2 + d], rx.at[h, 2 + d], at_x(around(x, step)))

    def end_gated(h):
        for d in (0, 1):
            got(half_rows(around(x, 2), h, d), sx.at[h, 2 + d], rx.at[h, 2 + d])

    def emit(i, q):
        panel = jnp.concatenate(
            [G[heads + i, a, q].reshape(-1, 2 * HDIM) for a in (0, 1)], axis=1
        )
        for lo in range(0, extent, BR):
            left = jnp.concatenate(
                [gall[2 * i + a, 2 * q + b, pl.ds(lo, BR)] for a in (0, 1) for b in (0, 1)], axis=1
            )
            acc[pl.ds(lo, BR)] += nt_dot(left, panel)

    def turn(t, carry):
        odd = rem(t, 2) == 1
        @pl.when(odd & (t <= 5))
        def _():
            first_end(div(t + 3, 2))
        @pl.when(odd & (t <= 3))
        def _():
            first_pass(div(t + 5, 2))
        @pl.when(t == 1)
        def _():
            first_send(4)
        @pl.when(t + 3 < steps)
        def _():
            second_send(t + 3)
        @pl.when(t + 1 < steps)
        def _():
            second_pass(t + 1)
        @pl.when((t >= 1) & (t - 1 < steps))
        def _():
            second_end(t - 1)
            share(t - 1)
        @pl.when((t >= 5) & (t - 5 < heads))
        def _():
            pass_gated(t - 5)
        @pl.when((t >= 4) & (t - 4 < heads))
        def _():
            finish(t - 4)
        @pl.when((t >= 3) & (t - 3 < heads))
        def _():
            gather_states(t - 3)
        @pl.when((t >= 2) & (t - 2 < steps))
        def _():
            shared(t - 2)
        @pl.when((t >= 2) & (t - 2 < heads))
        def _():
            project(t - 2)
        @pl.when((t >= 6) & (t - 6 < heads))
        def _():
            end_gated(t - 6)
        @pl.when(t >= heads + 2)
        def _():
            i = t - heads - 2
            def add(q, carry):
                emit(i, q)
                return carry
            lax.fori_loop(0, 2, add, 0)
        return carry

    lax.fori_loop(0, steps + 2, turn, 0)
    pass_gated(heads - 1)
    end_gated(heads - 2)
    lax.fori_loop(0, 2, lambda i, carry: (emit(i, 2), carry)[1], 0)
    end_gated(heads - 1)
    lax.fori_loop(0, 2, lambda i, carry: (emit(i, 3), carry)[1], 0)
    out[...] = acc[...].astype(out.dtype)

    def drain1(m, carry):
        for a in (0, 1):
            k, _ = first_ring[a]
            for d in (0, 1):
                sent(unit1(m, a, k), s1.at[m, a, d], r1.at[m, a, d])
                sent(unit1(m, a, k, 0, half), s1.at[m, a, 2 + d], r1.at[m, a, 2 + d])
        return carry

    def drain2(t, carry):
        for a in (0, 1):
            k, _ = second_ring[a]
            for d in (0, 1):
                sent(unit2(t, a, k), s2.at[t, a, d], r2.at[t, a, d])
                sent(half2(t, a, k, 0), s2.at[t, a, 2 + d], r2.at[t, a, 2 + d])
        sent(G.at[t, :, :, :, c], ssib.at[t], rsib.at[t])
        return carry

    def drain3(h, carry):
        for d in range(3):
            sent(lbuf.at[h, g], sl.at[h, d], rl.at[h, d])
            sent(tbuf.at[h, y], st.at[h, d], rt.at[h, d])
        for d in (0, 1):
            sent(gall.at[x, h], sx.at[h, d], rx.at[h, d])
            sent(half_rows(x, h, 0), sx.at[h, 2 + d], rx.at[h, 2 + d])
        return carry

    lax.fori_loop(0, pieces, drain1, 0)
    lax.fori_loop(0, steps, drain2, 0)
    lax.fori_loop(0, heads, drain3, 0)
    for q in range(4):
        @pl.when(jnp.logical_not(corner & (y == q)))
        def _():
            sent(out_unit(x, q), sa.at[q], ra.at[q])


def local(tokens, in_panels, out_panel, decay_power, boundary):
    slab_rows = tokens[0]
    extent, depth = slab_rows.shape
    seq_count = lax.axis_size("seq")
    own = lax.axis_index("seq")
    prompt_start = boundary[0]
    heads = decay_power.shape[0]
    rows = in_panels.shape[0]
    log_rate = log_half * jnp.exp2(decay_power.astype(F32)) / (extent * seq_count)

    shard = in_panels.reshape(rows, 2, 2, heads, HDIM).transpose(3, 1, 0, 2, 4)
    shard = shard.reshape(heads, 2, rows, 2 * HDIM)
    out_shard = out_panel.T

    crossing = prompt_start // extent

    def left(k, p):
        clear = (k < p) & ~((k < crossing) & (crossing < p))
        span = extent * jnp.maximum(p - 1 - k, 0).astype(F32)
        return jnp.where(clear[None], jnp.exp(log_rate[:, None] * span[None]), 0.0)

    four = jnp.arange(4, dtype=jnp.int32)
    base = own // 4 * 4
    coef = jnp.concatenate(
        [
            left(base + four, base + 4),
            left(base + four, own),
            left(4 * four + 3, own),
            jnp.exp(log_rate)[:, None],
            jnp.exp(log_rate * (extent - 1))[:, None],
            jnp.zeros((heads, 2), F32),
        ],
        axis=1,
    )
    place = (prompt_start - own * extent)[None]

    any_space = pl.BlockSpec(memory_space=pl.ANY)
    smem = pl.BlockSpec(memory_space=pltpu.SMEM)
    dma = pltpu.SemaphoreType.DMA
    steps = heads + 2
    columns = out_panel.shape[1] * 8
    result = pl.pallas_call(
        functools.partial(kernel, heads),
        out_shape=jax.ShapeDtypeStruct((extent, columns), BF16),
        in_specs=[smem, smem, smem, any_space, any_space, any_space],
        out_specs=pl.BlockSpec(memory_space=pltpu.VMEM),
        scratch_shapes=[
            pltpu.VMEM((steps, 2, 4, 2, 2, 2, rows, 2 * HDIM), BF16),
            pltpu.VMEM((extent, depth), BF16),
            pltpu.VMEM((4, heads, extent, HDIM), BF16),
            pltpu.VMEM((4, extent, HDIM), BF16),
            pltpu.VMEM((4, extent, HDIM), F32),
            pltpu.VMEM((4, extent, HDIM), F32),
            pltpu.VMEM((4, HDIM, HDIM), F32),
            pltpu.VMEM((heads, 4, HDIM, HDIM), BF16),
            pltpu.VMEM((heads, 4, HDIM, HDIM), BF16),
            pltpu.VMEM((extent, columns), F32),
            dma((3,)),
            dma((steps // 2, 2, 4)),
            dma((steps // 2, 2, 4)),
            dma((steps, 2, 4)),
            dma((steps, 2, 4)),
            dma((steps,)),
            dma((steps,)),
            dma((4,)),
            dma((4,)),
            dma((heads, 3)),
            dma((heads, 3)),
            dma((heads, 3)),
            dma((heads, 3)),
            dma((heads, 4)),
            dma((heads, 4)),
        ],
        compiler_params=pltpu.CompilerParams(
            collective_id=0, has_side_effects=True, vmem_limit_bytes=60 * 1024 * 1024
        ),
        cost_estimate=pl.CostEstimate(
            flops=2 * extent * depth * 4 * heads * HDIM, bytes_accessed=8_000_000, transcendentals=0
        ),
    )(log_rate, coef, place, slab_rows, shard, out_shard)
    return result[None]


def solution(mesh):
    return jax.shard_map(
        local,
        mesh=mesh,
        in_specs=(
            P("rep", "seq", None),
            P(("seq", "rep"), None, "tp"),
            P("tp", ("seq", "rep")),
            P("tp"),
            P("rep"),
        ),
        out_specs=P("rep", "seq", "tp"),
        check_vma=False,
    )
```

time: 411 us -> 153 us (0.37)
  waiting for transfers between devices: 295 us -> 0 us
  Pallas kernels: 0 us -> 144 us
  matrix products: 62.2 us -> 0 us
  local copies, waits for them, and re-layouts: 29.8 us -> 6.98 us
  between operations: 13.9 us -> 0.74 us
  other arithmetic: 8.14 us -> 0.79 us
    all_gather x3 -> x0, waiting for transfers between devices: 241 us -> none  [the longest x1 144 us: local(): full_in = lax.all_gather(flat_in, ('seq', 'rep'), axis=0, tiled=True)]
    pallas_call x0 -> x1, Pallas kernels: none -> 144 us  [local(): pl.pallas_call(functools.partial(kernel, heads), out_shape=jax.ShapeDtype...]
    dot_general x5 -> x0, matrix products: 62.2 us -> none  [the longest x1 26 us: local(): projected = jnp.dot(slab_rows, full_in, preferred_element_type=jnp.float32)]
    reduce_scatter x1 -> x0, waiting for transfers between devices: 52.9 us -> none  [local(): lax.psum_scatter(head_partial.astype(jnp.bfloat16), 'tp', scatter_dimensi...]
    unnamed x8 -> x3, local copies, waits for them, and re-layouts: 19.6 us -> 2.36 us
    slice x2 -> x0, local copies, waits for them, and re-layouts: 10.2 us -> none  [the longest x1 6.98 us: local(): gate_rows = jax.nn.sigmoid(projected[:, 3])]
  transfers between devices with their start and end apart: 4 -> 0, of which waited for: 4 -> 0; matrix products, arithmetic and copies ran while one was open for 8% -> 0% of each run, Pallas kernels for 0% -> 0%
where the time goes in v2:
time: 153 us
  Pallas kernels  144 us (94%)
  local copies, waits for them, and re-layouts  6.98 us (5%)
    pallas_call x1, Pallas kernels, local(): pl.pallas_call(functools.partial(kernel, heads), out_shape=jax.ShapeDtype...  144 us

profile of v2, /device:TPU:32, one launch (start us, length us, event | category | flops | bytes accessed | tf_op | source)
XLA Modules:
  0.0 152.6 jit_solution(6399720577605237137)
XLA Ops:
  0.7 0.7 exponential_bitcast_fusion
  1.4 0.0 copy-start
  1.4 0.1 copy.7
  1.5 0.1 copy.6
  1.6 0.1 exponential_select_fusion
  1.7 0.7 concatenate.3.coef
  2.3 1.6 %reshape.50 = bf16[96,2,2,8,128]{4,3,2,1,0:T(8,128)(2,1)S(1)} reshape(bf16[96,4,1024]{2,1,0:T(4,128)(2,1)} %param.6) | data formatting | bytes 1572864 | tf_op jit(solution)/shard_map/reshape | solution.py:406
  4.0 0.8 copy.10
  4.7 0.0 copy-done
  4.8 1.4 reshape.51.wsh
  6.1 144.1 %shard_map.55 = bf16[768,768]{1,0:T(8,128)(2,1)} custom-call(f32[8]{0:T(128)} %copy-done, f32[8,16]{1,0:T(8,128)} %concatenate.3.coef, s32[1]{0:T(128)} %bitcast.3.place, bf16[768,3072]{1,0:T(8,128)(2,1)} %bitcast.18, bf16[8,2,96,256]{3,2,1,0:T(8,128)(2,1)} %reshape.51.wsh, bf16[96,1024]{1,0:T(8,128)(2,1)} %bitcast.19), custom_call_target="tpu_custom_call" | custom-call | flops 19327352832 | bytes 8000000 | tf_op jit(solution)/shard_map/pallas_call | solution.py:437
  150.2 2.4 %copy.13 = bf16[1,768,768]{2,1,0:T(8,128)(2,1)} copy(bf16[1,768,768]{2,1,0:T(8,128)(2,1)} %bitcast.17) | data formatting | bytes 2359296
  (5 shorter events, 0.0 us)
Async XLA Ops:
  1.4 3.3 %copy-start = (f32[8]{0:T(128)}, f32[8]{0:T(128)S(1)}, u32[]{:S(2)}) copy-start(f32[8]{0:T(128)S(1)} %get-tuple-element.7.rates) | copy-start | bytes 100

commit v3 on v2

v3 whole, which is shorter than its diff:
```python
import functools

import jax
import jax.numpy as jnp
from jax import lax
from jax.experimental import pallas as pl
from jax.experimental.pallas import tpu as pltpu
from jax.sharding import PartitionSpec as P

HDIM = 128
MESH = pl.DeviceIdType.MESH
log_half = -0.6931471805599453
epsilon = 1e-06
F32 = jnp.float32
BF16 = jnp.bfloat16


def nt_dot(a, b):
    return lax.dot_general(a, b, (((1,), (1,)), ((), ())), preferred_element_type=F32)


def tn_dot(a, b):
    return lax.dot_general(a, b, (((0,), (0,)), ((), ())), preferred_element_type=F32)


def kernel(
    heads, rates, coef, place, tok, wsh, osh, out,
    G, tokv, gall, qbuf, wbuf, gbuf, lout, lbuf, tbuf, eout, ebuf, acc, stage,
    loc, s1, r1, s2, r2, ssib, rsib, sa, ra, sl, rl, st, rt, se, re, sx, rx,
):
    extent = tok.shape[0]
    rows = wsh.shape[2]
    half = rows // 2
    steps = heads + 2
    rem, div = lax.rem, lax.div
    s, x, zhi = lax.axis_index("seq"), lax.axis_index("tp"), lax.axis_index("rep")
    y, g, zlo, c = div(s, 4), rem(s, 4), rem(div(s, 2), 2), rem(s, 2)
    z = zhi * 2 + zlo

    def around(k, d):
        return rem(k + d, 4)

    def at_y(k):
        return {"seq": k * 4 + g}

    def at_z(k):
        return {"seq": y * 4 + rem(k, 2) * 2 + c, "rep": div(k, 2)}

    def at_g(k):
        return {"seq": y * 4 + k}

    def at_x(k):
        return {"tp": k}

    sibling = {"seq": y * 4 + zlo * 2 + 1 - c}

    barrier = pltpu.get_barrier_semaphore()

    def greet(device):
        pl.semaphore_signal(barrier, inc=1, device_id=device, device_id_type=MESH)

    own_copies = [
        pltpu.make_async_copy(tok, tokv, loc.at[0]),
        pltpu.make_async_copy(wsh, G.at[pl.ds(0, heads), :, y, zlo, c, zhi], loc.at[1]),
        pltpu.make_async_copy(osh.at[y], stage.at[y], loc.at[2]),
    ]
    own_copies[1].start()
    own_copies[2].start()
    for d in (1, 2, 3):
        greet(at_y(around(y, d)))
        greet(at_g(around(g, d)))
        greet(at_x(around(x, d)))
    for d in (1, 3):
        greet(at_z(around(z, d)))
    pl.semaphore_wait(barrier, 11)

    def send(src, dst, ss, rs, device):
        pltpu.make_async_remote_copy(
            src_ref=src, dst_ref=dst, send_sem=ss, recv_sem=rs, device_id=device, device_id_type=MESH
        ).start()

    def got(ref, ss, rs):
        pltpu.make_async_remote_copy(
            src_ref=ref, dst_ref=ref, send_sem=ss, recv_sem=rs, device_id=sibling, device_id_type=MESH
        ).wait_recv()

    def sent(ref, ss, rs):
        pltpu.make_async_remote_copy(
            src_ref=ref, dst_ref=ref, send_sem=ss, recv_sem=rs, device_id=sibling, device_id_type=MESH
        ).wait_send()

    first_ring = ((y, at_y), (z, at_z))
    second_ring = ((z, at_z), (y, at_y))

    def unit1(m, a, k, lo=0, n=rows):
        if a == 0:
            return G.at[m, 0, k, zlo, c, zhi, pl.ds(lo, n)]
        return G.at[m, 1, y, rem(k, 2), c, div(k, 2), pl.ds(lo, n)]

    def unit2(t, a, k):
        if a == 0:
            return G.at[t, 0, :, rem(k, 2), c, div(k, 2)]
        return G.at[t, 1, k, :, c]

    def half2(t, a, k, part):
        if a == 0:
            return G.at[t, 0, pl.ds(2 * part, 2), rem(k, 2), c, div(k, 2)]
        return G.at[t, 1, k, pl.ds(part, 1), c]

    SLOTS = 4

    def slot_of(m):
        return rem(m, SLOTS)

    def reused(m, wait):
        if isinstance(m, int):
            if m >= SLOTS:
                wait()
        else:
            pl.when(m >= SLOTS)(wait)

    def first_sent(k):
        sent(G.at[0, 0, pl.ds(0, 3), :, 0, 0], s1.at[k], s1.at[k])

    def second_sent(k):
        sent(G.at[0, 0, pl.ds(0, 3)], s2.at[k], s2.at[k])

    def first_send(m):
        k0 = slot_of(m)
        reused(m, lambda: first_sent(k0))
        for a in (0, 1):
            k, at = first_ring[a]
            own = unit1(m, a, k)
            for d, step in ((0, 1), (1, 3)):
                send(own, own, s1.at[k0], r1.at[k0, a, d], at(around(k, step)))

    def first_pass(m):
        k0 = slot_of(m)
        for a in (0, 1):
            k, at = first_ring[a]
            for d, step in ((0, 1), (1, 3)):
                origin = around(k, 4 - step)
                got(unit1(m, a, origin), s1.at[k0], r1.at[k0, a, d])
                part = unit1(m, a, origin, d * half, half)
                send(part, part, s1.at[k0], r1.at[k0, a, 2], at(around(k, step)))

    def first_end(m):
        k0 = slot_of(m)
        for a in (0, 1):
            k, _ = first_ring[a]
            got(unit1(m, a, around(k, 2)), s1.at[k0], r1.at[k0, a, 2])

    def second_send(t):
        k0 = slot_of(t)
        reused(t, lambda: second_sent(k0))
        for a in (1, 0):
            k, at = second_ring[a]
            own = unit2(t, a, k)
            for d, step in ((0, 1), (1, 3)):
                send(own, own, s2.at[k0], r2.at[k0, a, d], at(around(k, step)))

    def second_pass(t):
        k0 = slot_of(t)
        for a in (1, 0):
            k, at = second_ring[a]
            for d, step in ((0, 1), (1, 3)):
                origin = around(k, 4 - step)
                got(unit2(t, a, origin), s2.at[k0], r2.at[k0, a, d])
                part = half2(t, a, origin, d)
                send(part, part, s2.at[k0], r2.at[k0, a, 2], at(around(k, step)))

    def second_end(t):
        k0 = slot_of(t)
        for a in (1, 0):
            k, _ = second_ring[a]
            got(unit2(t, a, around(k, 2)), s2.at[k0], r2.at[k0, a, 2])

    def share_sent(k):
        sent(G.at[0, :, :, :, c], ssib.at[k], ssib.at[k])

    def share(t):
        k0 = slot_of(t)
        reused(t, lambda: share_sent(k0))
        mine = G.at[t, :, :, :, c]
        send(mine, mine, ssib.at[k0], rsib.at[k0], sibling)

    def shared(t):
        k0 = slot_of(t)
        got(G.at[t, :, :, :, 1 - c], ssib.at[k0], rsib.at[k0])

    def out_unit(k, q):
        return G.at[heads + div(k, 2), rem(k, 2), q, zlo, c, zhi]

    def regroup_y():
        for d in (1, 2, 3):
            q = around(y, d)
            send(osh.at[q], stage.at[y], sa.at[0], ra.at[0], at_y(q))

    def regroup_x():
        own_copies[2].wait()
        got(stage.at[pl.ds(0, 3)], sa.at[0], ra.at[0])
        pltpu.make_async_copy(stage.at[x], out_unit(x, y), loc.at[2]).start()
        for d in (1, 2, 3):
            k = around(x, d)
            send(stage.at[k], out_unit(x, y), sa.at[1], ra.at[1], at_x(k))

    def regrouped():
        pltpu.make_async_copy(stage.at[x], out_unit(x, y), loc.at[2]).wait()
        got(stage.at[pl.ds(0, 3)], sa.at[1], ra.at[1])

    own_copies[1].wait()
    first_send(0)
    first_send(1)
    regroup_y()
    own_copies[0].start()
    first_pass(0)
    first_send(2)
    first_pass(1)
    first_end(0)
    second_send(0)
    first_pass(2)
    first_send(3)
    regroup_x()
    acc[...] = jnp.zeros_like(acc)
    own_copies[0].wait()

    edge = place[0]
    down = lax.broadcasted_iota(jnp.int32, (extent, HDIM), 0)
    BR = 256
    QR = HDIM // 4

    def blocks_sent(sem):
        sent(lbuf.at[0, pl.ds(0, 3)], sem, sem)

    def gated_sent(k):
        sent(gall.at[pl.ds(0, 3), 0], sx.at[k], sx.at[k])

    def project(h):
        slot = rem(h, 4)
        rate = rates[h]
        panel = G[h, 0].reshape(-1, 2 * HDIM)
        u = jnp.dot(tokv[...], panel, preferred_element_type=F32)
        down_f = down.astype(F32)
        grow = jnp.exp(rate * down_f)
        shrink = jnp.exp(-rate * down_f)
        uq, uk = u[:, :HDIM], u[:, HDIM:]
        q = ((uq / (1.0 + jnp.exp(-uq))) * (HDIM ** -0.5) * grow).astype(BF16)
        kf = (uk / (1.0 + jnp.exp(-uk))) * shrink
        k = kf.astype(BF16)
        kept = jnp.where((down >= edge) | (edge >= extent), kf, 0.0).astype(BF16)
        panel = G[h, 1].reshape(-1, 2 * HDIM)
        u = jnp.dot(tokv[...], panel, preferred_element_type=F32)
        v = u[:, :HDIM].astype(BF16)
        gbuf[slot] = 1.0 / (1.0 + jnp.exp(-u[:, HDIM:]))
        qbuf[slot] = q
        k0 = slot_of(h)
        reused(h, lambda: blocks_sent(sl.at[k0]))
        added = (tn_dot(kept, v) * coef[h, 37]).astype(BF16)
        lout[k0] = added
        lbuf[h, g] = lout[k0, pl.ds(g * QR, QR)]
        for d in (1, 2, 3):
            to = around(g, d)
            send(lout.at[k0, pl.ds(to * QR, QR)], lbuf.at[h, g], sl.at[k0], rl.at[k0], at_g(to))
        for lo in range(0, extent, BR):
            hi = lo + BR
            scores = nt_dot(q[lo:hi], k[:hi])
            i = lax.broadcasted_iota(jnp.int32, (BR, hi), 0) + lo
            j = lax.broadcasted_iota(jnp.int32, (BR, hi), 1)
            keep = (j <= i) & (j >= jnp.where(i >= edge, edge, 0))
            scores = jnp.where(keep, scores, 0.0).astype(BF16)
            wbuf[slot, pl.ds(lo, BR)] = jnp.dot(scores, v[:hi], preferred_element_type=F32)

    def gather_states(h):
        k0 = slot_of(h)
        got(lbuf.at[h, pl.ds(0, 3)], sl.at[k0], rl.at[k0])
        total = coef[h, 0] * lbuf[h, 0].astype(F32)
        for k in range(1, 4):
            total += coef[h, k] * lbuf[h, k].astype(F32)
        reused(h, lambda: blocks_sent(st.at[k0]))
        tbuf[h, y] = total.astype(BF16)
        for d in (1, 2, 3):
            own = tbuf.at[h, y]
            send(own, own, st.at[k0], rt.at[k0], at_y(around(y, d)))

    def spread_states(h):
        k0 = slot_of(h)
        got(tbuf.at[h, pl.ds(0, 3)], st.at[k0], rt.at[k0])
        reused(h, lambda: blocks_sent(se.at[k0]))
        for p in range(4):
            state = jnp.zeros((QR, HDIM), F32)
            for k in range(4):
                state += coef[h, 4 + 8 * p + k] * lbuf[h, k].astype(F32)
                state += coef[h, 8 + 8 * p + k] * tbuf[h, k].astype(F32)
            eout[k0, p] = state.astype(BF16)
        ebuf[h, g] = eout[k0, g]
        for d in (1, 2, 3):
            k = around(g, d)
            send(eout.at[k0, k], ebuf.at[h, g], se.at[k0], re.at[k0], at_g(k))

    def finish(h):
        slot = rem(h, 4)
        k0 = slot_of(h)
        got(ebuf.at[h, pl.ds(0, 3)], se.at[k0], re.at[k0])
        state = ebuf[h].reshape(HDIM, HDIM)
        use = jnp.where((down < edge) | (edge < 0), coef[h, 36], 0.0)
        across = jnp.dot(qbuf[slot], state, preferred_element_type=F32)
        attended = wbuf[slot] + across * use
        square = jnp.mean(attended * attended, axis=-1, keepdims=True)
        gall[x, h] = (attended * lax.rsqrt(square + epsilon) * gbuf[slot]).astype(BF16)
        reused(h, lambda: gated_sent(k0))
        own = gall.at[x, h]
        for d, step in ((0, 1), (1, 3)):
            send(own, own, sx.at[k0], rx.at[k0, d], at_x(around(x, step)))

    def half_rows(k, h, d):
        return gall.at[k, h, pl.ds(d * (extent // 2), extent // 2)]

    def pass_gated(h):
        k0 = slot_of(h)
        for d, step in ((0, 1), (1, 3)):
            origin = around(x, 4 - step)
            got(gall.at[origin, h], sx.at[k0], rx.at[k0, d])
            part = half_rows(origin, h, d)
            send(part, part, sx.at[k0], rx.at[k0, 2], at_x(around(x, step)))

    def end_gated(h):
        k0 = slot_of(h)
        got(gall.at[around(x, 2), h], sx.at[k0], rx.at[k0, 2])

    def emit(i, q):
        panel = jnp.concatenate(
            [G[heads + i, a, q].reshape(-1, 2 * HDIM) for a in (0, 1)], axis=1
        )
        for lo in range(0, extent, BR):
            left = jnp.concatenate(
                [gall[2 * i + a, 2 * q + b, pl.ds(lo, BR)] for a in (0, 1) for b in (0, 1)], axis=1
            )
            acc[pl.ds(lo, BR)] += nt_dot(left, panel)

    def turn(n, carry):
        t = n - 1

        def when(lag, count):
            return pl.when((t >= lag) & (t - lag < count))

        @when(-1, steps)
        def _():
            second_pass(t + 1)
        @when(2, heads)
        def _():
            finish(t - 2)
        @when(1, heads)
        def _():
            gather_states(t - 1)
        @pl.when(t + 2 < steps)
        def _():
            first_end(t + 2)
            second_send(t + 2)
        @pl.when(t + 4 < steps)
        def _():
            first_pass(t + 4)
        @pl.when(t + 5 == heads)
        def _():
            regrouped()
        @pl.when(t + 5 < steps)
        def _():
            first_send(t + 5)
        @when(0, steps)
        def _():
            shared(t)
        @when(0, heads)
        def _():
            project(t)
        @when(1, heads)
        def _():
            spread_states(t - 1)
        @when(2, heads)
        def _():
            pass_gated(t - 2)
        @when(-1, steps)
        def _():
            second_end(t + 1)
            share(t + 1)
        @when(3, heads)
        def _():
            end_gated(t - 3)
        @when(heads, 2)
        def _():
            def add(q, carry):
                emit(t - heads, q)
                return carry
            lax.fori_loop(0, 2, add, 0)
        return carry

    lax.fori_loop(0, steps + 1, turn, 0)

    def both(q):
        lax.fori_loop(0, 2, lambda i, carry: (emit(i, q), carry)[1], 0)

    both(2)
    end_gated(heads - 1)
    both(3)
    out[...] = acc[...].astype(out.dtype)

    for k in range(SLOTS):
        first_sent(k)
        second_sent(k)
        share_sent(k)
        blocks_sent(sl.at[k])
        blocks_sent(st.at[k])
        blocks_sent(se.at[k])
        gated_sent(k)
    for k in range(2):
        sent(stage.at[pl.ds(0, 3)], sa.at[k], sa.at[k])


def local(tokens, in_panels, out_panel, decay_power, boundary):
    slab_rows = tokens[0]
    extent, depth = slab_rows.shape
    seq_count = lax.axis_size("seq")
    own = lax.axis_index("seq")
    prompt_start = boundary[0]
    heads = decay_power.shape[0]
    rows = in_panels.shape[0]
    log_rate = log_half * jnp.exp2(decay_power.astype(F32)) / (extent * seq_count)

    shard = in_panels.reshape(rows, 2, 2, heads, HDIM).transpose(3, 1, 0, 2, 4)
    shard = shard.reshape(heads, 2, rows, 2 * HDIM)
    out_shard = out_panel.T.reshape(rows, 4, -1).transpose(1, 0, 2)

    crossing = prompt_start // extent

    def left(k, p):
        clear = (k < p) & ~((k < crossing) & (crossing < p))
        span = extent * jnp.maximum(p - 1 - k, 0).astype(F32)
        return jnp.where(clear[None], jnp.exp(log_rate[:, None] * span[None]), 0.0)

    four = jnp.arange(4, dtype=jnp.int32)
    base = own // 4 * 4
    coef = jnp.concatenate(
        [
            left(base + four, base + 4),
            *[
                left(origin, base + k)
                for k in range(4)
                for origin in (base + four, 4 * four + 3)
            ],
            jnp.exp(log_rate)[:, None],
            jnp.exp(log_rate * (extent - 1))[:, None],
        ],
        axis=1,
    )
    place = (prompt_start - own * extent)[None]

    any_space = pl.BlockSpec(memory_space=pl.ANY)
    smem = pl.BlockSpec(memory_space=pltpu.SMEM)
    dma = pltpu.SemaphoreType.DMA
    steps = heads + 2
    columns = out_panel.shape[1] * 8
    result = pl.pallas_call(
        functools.partial(kernel, heads),
        out_shape=jax.ShapeDtypeStruct((extent, columns), BF16),
        in_specs=[smem, smem, smem, any_space, any_space, any_space],
        out_specs=pl.BlockSpec(memory_space=pltpu.VMEM),
        scratch_shapes=[
            pltpu.VMEM((steps, 2, 4, 2, 2, 2, rows, 2 * HDIM), BF16),
            pltpu.VMEM((extent, depth), BF16),
            pltpu.VMEM((4, heads, extent, HDIM), BF16),
            pltpu.VMEM((4, extent, HDIM), BF16),
            pltpu.VMEM((4, extent, HDIM), F32),
            pltpu.VMEM((4, extent, HDIM), F32),
            pltpu.VMEM((4, HDIM, HDIM), BF16),
            pltpu.VMEM((heads, 4, HDIM // 4, HDIM), BF16),
            pltpu.VMEM((heads, 4, HDIM // 4, HDIM), BF16),
            pltpu.VMEM((4, 4, HDIM // 4, HDIM), BF16),
            pltpu.VMEM((heads, 4, HDIM // 4, HDIM), BF16),
            pltpu.VMEM((extent, columns), F32),
            pltpu.VMEM((4, out_panel.shape[1], out_panel.shape[0] // 4), BF16),
            dma((3,)),
            dma((4,)),
            dma((4, 2, 3)),
            dma((4,)),
            dma((4, 2, 3)),
            dma((4,)),
            dma((4,)),
            dma((2,)),
            dma((2,)),
            dma((4,)),
            dma((4,)),
            dma((4,)),
            dma((4,)),
            dma((4,)),
            dma((4,)),
            dma((4,)),
            dma((4, 3)),
        ],
        compiler_params=pltpu.CompilerParams(
            collective_id=0, has_side_effects=True, vmem_limit_bytes=60 * 1024 * 1024
        ),
        cost_estimate=pl.CostEstimate(
            flops=2 * extent * depth * 4 * heads * HDIM, bytes_accessed=8_000_000, transcendentals=0
        ),
    )(log_rate, coef, place, slab_rows, shard, out_shard)
    return result[None]


def solution(mesh):
    return jax.shard_map(
        local,
        mesh=mesh,
        in_specs=(
            P("rep", "seq", None),
            P(("seq", "rep"), None, "tp"),
            P("tp", ("seq", "rep")),
            P("tp"),
            P("rep"),
        ),
        out_specs=P("rep", "seq", "tp"),
        check_vma=False,
    )
```

time: 153 us -> 133 us (0.87)
  Pallas kernels: 144 us -> 122 us
  local copies, waits for them, and re-layouts: 6.98 us -> 8.61 us
    pallas_call x1, Pallas kernels: 144 us -> 122 us  [local(): pl.pallas_call(functools.partial(kernel, heads), out_shape=jax.ShapeDtype...]
    reshape x0 -> x1, local copies, waits for them, and re-layouts: none -> 1.63 us  [local(): out_shard = out_panel.T.reshape(rows, 4, -1).transpose(1, 0, 2)]
where the time goes in v3:
time: 133 us; the launch traced here: 132 us
  Pallas kernels  122 us (92%)
  local copies, waits for them, and re-layouts  8.61 us (6%)
    pallas_call x1, Pallas kernels, local(): pl.pallas_call(functools.partial(kernel, heads), out_shape=jax.ShapeDtype...  122 us

profile of v3, /device:TPU:32, one launch (start us, length us, event | category | flops | bytes accessed | tf_op | source)
XLA Modules:
  0.0 131.8 jit_solution(2916191694340155970)
XLA Ops:
  0.9 0.7 exponential_bitcast_fusion
  1.5 0.0 copy-start
  1.5 0.1 copy.10
  1.6 0.1 copy.9
  1.7 0.1 exponential_select_fusion
  1.8 0.7 concatenate.3.coef
  2.5 1.6 %copy.17 = bf16[12,4,8,256]{3,2,0,1:T(8,128)(2,1)} copy(bf16[12,4,8,256]{3,2,1,0:T(8,128)(2,1)} %bitcast.25) | data formatting | bytes 393216 | tf_op jit(solution)/shard_map/reshape | solution.py:429
  4.1 1.6 %reshape.125 = bf16[96,2,2,8,128]{4,3,2,1,0:T(8,128)(2,1)S(1)} reshape(bf16[96,4,1024]{2,1,0:T(4,128)(2,1)} %param.6) | data formatting | bytes 1572864 | tf_op jit(solution)/shard_map/reshape | solution.py:427
  5.7 0.8 copy.16
  6.5 0.0 copy-done
  6.5 1.4 %reshape.126.wsh = bf16[8,2,96,256]{3,2,1,0:T(8,128)(2,1)} reshape(bf16[8,2,96,2,128]{4,3,2,1,0:T(2,128)(2,1)S(1)} %bitcast.23) | data formatting | bytes 1572864 | tf_op jit(solution)/shard_map/reshape | solution.py:428
  7.9 121.6 %shard_map.55 = bf16[768,768]{1,0:T(8,128)(2,1)} custom-call(f32[8]{0:T(128)} %copy-done, f32[8,38]{1,0:T(8,128)} %concatenate.3.coef, s32[1]{0:T(128)} %bitcast.3.place, bf16[768,3072]{1,0:T(8,128)(2,1)} %bitcast.27, bf16[8,2,96,256]{3,2,1,0:T(8,128)(2,1)} %reshape.126.wsh, bf16[4,96,256]{2,1,0:T(8,128)(2,1)} %bitcast.26), custom_call_target="tpu_custom_call" | custom-call | flops 19327352832 | bytes 8000000 | tf_op jit(solution)/shard_map/pallas_call | solution.py:460
  129.5 2.4 %copy.20 = bf16[1,768,768]{2,1,0:T(8,128)(2,1)} copy(bf16[1,768,768]{2,1,0:T(8,128)(2,1)} %bitcast.24) | data formatting | bytes 2359296
  (10 shorter events, 0.1 us)
Async XLA Ops:
  1.5 5.0 %copy-start = (f32[8]{0:T(128)}, f32[8]{0:T(128)S(1)}, u32[]{:S(2)}) copy-start(f32[8]{0:T(128)S(1)} %get-tuple-element.7.rates) | copy-start | bytes 100

commit v4 on v3

--- a/solution.py
+++ b/solution.py
@@ -24,7 +24,7 @@
 
 
 def kernel(
-    heads, rates, coef, place, tok, wsh, osh, out,
+    heads, blocks, powers, place, tok, wsh, osh, out,
     G, tokv, gall, qbuf, wbuf, gbuf, lout, lbuf, tbuf, eout, ebuf, acc, stage,
     loc, s1, r1, s2, r2, ssib, rsib, sa, ra, sl, rl, st, rt, se, re, sx, rx,
 ):
@@ -59,10 +59,14 @@
     def greet(device):
         pl.semaphore_signal(barrier, inc=1, device_id=device, device_id_type=MESH)
 
+    def quarter(q):
+        width = osh.shape[1] // 4
+        return osh.at[:, pl.ds(pl.multiple_of(q * width, width), width)]
+
     own_copies = [
         pltpu.make_async_copy(tok, tokv, loc.at[0]),
         pltpu.make_async_copy(wsh, G.at[pl.ds(0, heads), :, y, zlo, c, zhi], loc.at[1]),
-        pltpu.make_async_copy(osh.at[y], stage.at[y], loc.at[2]),
+        pltpu.make_async_copy(quarter(y), stage.at[y], loc.at[2]),
     ]
     own_copies[1].start()
     own_copies[2].start()
@@ -131,8 +135,9 @@
         for a in (0, 1):
             k, at = first_ring[a]
             own = unit1(m, a, k)
+            start = wsh.at[m, a] if isinstance(m, int) else own
             for d, step in ((0, 1), (1, 3)):
-                send(own, own, s1.at[k0], r1.at[k0, a, d], at(around(k, step)))
+                send(start, own, s1.at[k0], r1.at[k0, a, d], at(around(k, step)))
 
     def first_pass(m):
         k0 = slot_of(m)
@@ -150,29 +155,28 @@
             k, _ = first_ring[a]
             got(unit1(m, a, around(k, 2)), s1.at[k0], r1.at[k0, a, 2])
 
-    def second_send(t):
+    def second_send_one(t, a, d):
         k0 = slot_of(t)
-        reused(t, lambda: second_sent(k0))
-        for a in (1, 0):
-            k, at = second_ring[a]
-            own = unit2(t, a, k)
-            for d, step in ((0, 1), (1, 3)):
-                send(own, own, s2.at[k0], r2.at[k0, a, d], at(around(k, step)))
-
-    def second_pass(t):
+        k, at = second_ring[a]
+        for n in (0, 1):
+            own = half2(t, a, k, (d + n) % 2)
+            send(own, own, s2.at[k0], r2.at[k0, a, d + 3 * n], at(around(k, 3 if d else 1)))
+
+    def second_pass_one(t, a, d):
         k0 = slot_of(t)
-        for a in (1, 0):
-            k, at = second_ring[a]
-            for d, step in ((0, 1), (1, 3)):
-                origin = around(k, 4 - step)
-                got(unit2(t, a, origin), s2.at[k0], r2.at[k0, a, d])
-                part = half2(t, a, origin, d)
-                send(part, part, s2.at[k0], r2.at[k0, a, 2], at(around(k, step)))
+        k, at = second_ring[a]
+        step = 3 if d else 1
+        origin = around(k, 4 - step)
+        part = half2(t, a, origin, d)
+        got(part, s2.at[k0], r2.at[k0, a, d])
+        send(part, part, s2.at[k0], r2.at[k0, a, 2], at(around(k, step)))
 
     def second_end(t):
         k0 = slot_of(t)
         for a in (1, 0):
             k, _ = second_ring[a]
+            for d in (0, 1):
+                got(half2(t, a, k, d), s2.at[k0], r2.at[k0, a, 3 + d])
             got(unit2(t, a, around(k, 2)), s2.at[k0], r2.at[k0, a, 2])
 
     def share_sent(k):
@@ -194,7 +198,7 @@
     def regroup_y():
         for d in (1, 2, 3):
             q = around(y, d)
-            send(osh.at[q], stage.at[y], sa.at[0], ra.at[0], at_y(q))
+            send(quarter(q), stage.at[y], sa.at[0], ra.at[0], at_y(q))
 
     def regroup_x():
         own_copies[2].wait()
@@ -208,23 +212,37 @@
         pltpu.make_async_copy(stage.at[x], out_unit(x, y), loc.at[2]).wait()
         got(stage.at[pl.ds(0, 3)], sa.at[1], ra.at[1])
 
-    own_copies[1].wait()
     first_send(0)
     first_send(1)
+    first_send(2)
     regroup_y()
     own_copies[0].start()
     first_pass(0)
-    first_send(2)
+    own_copies[1].wait()
     first_pass(1)
     first_end(0)
-    second_send(0)
+    for a in (0, 1):
+        for d in (0, 1):
+            second_send_one(0, a, d)
     first_pass(2)
     first_send(3)
     regroup_x()
     acc[...] = jnp.zeros_like(acc)
     own_copies[0].wait()
 
-    edge = place[0]
+    edge = place[0] - s * extent
+    crossing = div(place[0], extent)
+    base = y * 4
+
+    def rate_of(h):
+        return (log_half / (extent * blocks)) * jnp.left_shift(1, powers[h]).astype(F32)
+
+    def left(h, k, p):
+        clear = (k < p) & jnp.logical_not((k < crossing) & (crossing < p))
+        span = (extent * jnp.maximum(p - 1 - k, 0)).astype(F32)
+        share = jnp.exp(jnp.full((8, HDIM), rate_of(h) * span, F32))[:1]
+        return jnp.where(clear, share, 0.0)
+
     down = lax.broadcasted_iota(jnp.int32, (extent, HDIM), 0)
     BR = 256
     QR = HDIM // 4
@@ -237,7 +255,7 @@
 
     def project(h):
         slot = rem(h, 4)
-        rate = rates[h]
+        rate = rate_of(h)
         panel = G[h, 0].reshape(-1, 2 * HDIM)
         u = jnp.dot(tokv[...], panel, preferred_element_type=F32)
         down_f = down.astype(F32)
@@ -255,7 +273,7 @@
         qbuf[slot] = q
         k0 = slot_of(h)
         reused(h, lambda: blocks_sent(sl.at[k0]))
-        added = (tn_dot(kept, v) * coef[h, 37]).astype(BF16)
+        added = (tn_dot(kept, v) * jnp.exp(jnp.full((8, HDIM), rate * (extent - 1), F32))[:1]).astype(BF16)
         lout[k0] = added
         lbuf[h, g] = lout[k0, pl.ds(g * QR, QR)]
         for d in (1, 2, 3):
@@ -273,9 +291,9 @@
     def gather_states(h):
         k0 = slot_of(h)
         got(lbuf.at[h, pl.ds(0, 3)], sl.at[k0], rl.at[k0])
-        total = coef[h, 0] * lbuf[h, 0].astype(F32)
-        for k in range(1, 4):
-            total += coef[h, k] * lbuf[h, k].astype(F32)
+        total = jnp.zeros((QR, HDIM), F32)
+        for k in range(4):
+            total += left(h, base + k, base + 4) * lbuf[h, k].astype(F32)
         reused(h, lambda: blocks_sent(st.at[k0]))
         tbuf[h, y] = total.astype(BF16)
         for d in (1, 2, 3):
@@ -289,8 +307,9 @@
         for p in range(4):
             state = jnp.zeros((QR, HDIM), F32)
             for k in range(4):
-                state += coef[h, 4 + 8 * p + k] * lbuf[h, k].astype(F32)
-                state += coef[h, 8 + 8 * p + k] * tbuf[h, k].astype(F32)
+                if k < p:
+                    state += left(h, base + k, base + p) * lbuf[h, k].astype(F32)
+                state += left(h, 4 * k + 3, base + p) * tbuf[h, k].astype(F32)
             eout[k0, p] = state.astype(BF16)
         ebuf[h, g] = eout[k0, g]
         for d in (1, 2, 3):
@@ -302,15 +321,17 @@
         k0 = slot_of(h)
         got(ebuf.at[h, pl.ds(0, 3)], se.at[k0], re.at[k0])
         state = ebuf[h].reshape(HDIM, HDIM)
-        use = jnp.where((down < edge) | (edge < 0), coef[h, 36], 0.0)
+        once = jnp.exp(jnp.full((8, HDIM), rate_of(h), F32))[:1]
+        use = jnp.where((down < edge) | (edge < 0), once, 0.0)
         across = jnp.dot(qbuf[slot], state, preferred_element_type=F32)
         attended = wbuf[slot] + across * use
         square = jnp.mean(attended * attended, axis=-1, keepdims=True)
         gall[x, h] = (attended * lax.rsqrt(square + epsilon) * gbuf[slot]).astype(BF16)
         reused(h, lambda: gated_sent(k0))
-        own = gall.at[x, h]
-        for d, step in ((0, 1), (1, 3)):
-            send(own, own, sx.at[k0], rx.at[k0, d], at_x(around(x, step)))
+        for n in (0, 1):
+            for d, step in ((0, 1), (1, 3)):
+                own = half_rows(x, h, (d + n) % 2)
+                send(own, own, sx.at[k0], rx.at[k0, d + 3 * n], at_x(around(x, step)))
 
     def half_rows(k, h, d):
         return gall.at[k, h, pl.ds(d * (extent // 2), extent // 2)]
@@ -319,12 +340,14 @@
         k0 = slot_of(h)
         for d, step in ((0, 1), (1, 3)):
             origin = around(x, 4 - step)
-            got(gall.at[origin, h], sx.at[k0], rx.at[k0, d])
             part = half_rows(origin, h, d)
+            got(part, sx.at[k0], rx.at[k0, d])
             send(part, part, sx.at[k0], rx.at[k0, 2], at_x(around(x, step)))
 
     def end_gated(h):
         k0 = slot_of(h)
+        for d in (0, 1):
+            got(half_rows(x, h, d), sx.at[k0], rx.at[k0, 3 + d])
         got(gall.at[around(x, 2), h], sx.at[k0], rx.at[k0, 2])
 
     def emit(i, q):
@@ -343,19 +366,46 @@
         def when(lag, count):
             return pl.when((t >= lag) & (t - lag < count))
 
+        @pl.when(t + 2 < steps)
+        def _():
+            first_end(t + 2)
+            reused(t + 2, lambda: second_sent(slot_of(t + 2)))
+
+        def ring(a, d):
+            @when(-1, steps)
+            def _():
+                second_pass_one(t + 1, a, d)
+
+        def own(a, d):
+            @pl.when(t + 2 < steps)
+            def _():
+                second_send_one(t + 2, a, d)
+
+        for d in (0, 1):
+            ring(0, d)
+            own(0, d)
+        ring(1, 0)
+        ring(1, 1)
+        @when(1, heads)
+        def _():
+            gather_states(t - 1)
+        own(1, 0)
+        own(1, 1)
+        @when(2, heads)
+        def _():
+            finish(t - 2)
+        @when(0, steps)
+        def _():
+            shared(t)
+        @when(0, heads)
+        def _():
+            project(t)
         @when(-1, steps)
         def _():
-            second_pass(t + 1)
-        @when(2, heads)
-        def _():
-            finish(t - 2)
-        @when(1, heads)
-        def _():
-            gather_states(t - 1)
-        @pl.when(t + 2 < steps)
-        def _():
-            first_end(t + 2)
-            second_send(t + 2)
+            second_end(t + 1)
+        @when(-1, steps)
+        def _():
+            share(t + 1)
         @pl.when(t + 4 < steps)
         def _():
             first_pass(t + 4)
@@ -365,31 +415,18 @@
         @pl.when(t + 5 < steps)
         def _():
             first_send(t + 5)
-        @when(0, steps)
-        def _():
-            shared(t)
-        @when(0, heads)
-        def _():
-            project(t)
         @when(1, heads)
         def _():
             spread_states(t - 1)
+        @pl.when(t == heads + 1)
+        def _():
+            lax.fori_loop(0, 4, lambda n, carry: (emit(div(n, 2), rem(n, 2)), carry)[1], 0)
         @when(2, heads)
         def _():
             pass_gated(t - 2)
-        @when(-1, steps)
-        def _():
-            second_end(t + 1)
-            share(t + 1)
         @when(3, heads)
         def _():
             end_gated(t - 3)
-        @when(heads, 2)
-        def _():
-            def add(q, carry):
-                emit(t - heads, q)
-                return carry
-            lax.fori_loop(0, 2, add, 0)
         return carry
 
     lax.fori_loop(0, steps + 1, turn, 0)
@@ -418,39 +455,11 @@
     slab_rows = tokens[0]
     extent, depth = slab_rows.shape
     seq_count = lax.axis_size("seq")
-    own = lax.axis_index("seq")
-    prompt_start = boundary[0]
     heads = decay_power.shape[0]
     rows = in_panels.shape[0]
-    log_rate = log_half * jnp.exp2(decay_power.astype(F32)) / (extent * seq_count)
-
     shard = in_panels.reshape(rows, 2, 2, heads, HDIM).transpose(3, 1, 0, 2, 4)
     shard = shard.reshape(heads, 2, rows, 2 * HDIM)
-    out_shard = out_panel.T.reshape(rows, 4, -1).transpose(1, 0, 2)
-
-    crossing = prompt_start // extent
-
-    def left(k, p):
-        clear = (k < p) & ~((k < crossing) & (crossing < p))
-        span = extent * jnp.maximum(p - 1 - k, 0).astype(F32)
-        return jnp.where(clear[None], jnp.exp(log_rate[:, None] * span[None]), 0.0)
-
-    four = jnp.arange(4, dtype=jnp.int32)
-    base = own // 4 * 4
-    coef = jnp.concatenate(
-        [
-            left(base + four, base + 4),
-            *[
-                left(origin, base + k)
-                for k in range(4)
-                for origin in (base + four, 4 * four + 3)
-            ],
-            jnp.exp(log_rate)[:, None],
-            jnp.exp(log_rate * (extent - 1))[:, None],
-        ],
-        axis=1,
-    )
-    place = (prompt_start - own * extent)[None]
+    out_shard = out_panel.T
 
     any_space = pl.BlockSpec(memory_space=pl.ANY)
     smem = pl.BlockSpec(memory_space=pltpu.SMEM)
@@ -458,9 +467,9 @@
     steps = heads + 2
     columns = out_panel.shape[1] * 8
     result = pl.pallas_call(
-        functools.partial(kernel, heads),
+        functools.partial(kernel, heads, seq_count),
         out_shape=jax.ShapeDtypeStruct((extent, columns), BF16),
-        in_specs=[smem, smem, smem, any_space, any_space, any_space],
+        in_specs=[smem, smem, any_space, any_space, any_space],
         out_specs=pl.BlockSpec(memory_space=pltpu.VMEM),
         scratch_shapes=[
             pltpu.VMEM((steps, 2, 4, 2, 2, 2, rows, 2 * HDIM), BF16),
@@ -480,7 +489,7 @@
             dma((4,)),
             dma((4, 2, 3)),
             dma((4,)),
-            dma((4, 2, 3)),
+            dma((4, 2, 5)),
             dma((4,)),
             dma((4,)),
             dma((2,)),
@@ -492,7 +501,7 @@
             dma((4,)),
             dma((4,)),
             dma((4,)),
-            dma((4, 3)),
+            dma((4, 5)),
         ],
         compiler_params=pltpu.CompilerParams(
             collective_id=0, has_side_effects=True, vmem_limit_bytes=60 * 1024 * 1024
@@ -500,7 +509,7 @@
         cost_estimate=pl.CostEstimate(
             flops=2 * extent * depth * 4 * heads * HDIM, bytes_accessed=8_000_000, transcendentals=0
         ),
-    )(log_rate, coef, place, slab_rows, shard, out_shard)
+    )(decay_power, boundary, slab_rows, shard, out_shard)
     return result[None]
 
 

time: 133 us -> 121 us (0.910)
  Pallas kernels: 122 us -> 113 us
  local copies, waits for them, and re-layouts: 8.61 us -> 6.15 us
    pallas_call x1, Pallas kernels: 122 us -> 113 us  [local(): pl.pallas_call(functools.partial(kernel, heads, seq_count), out_shape=jax...]
    reshape x1 -> x0, local copies, waits for them, and re-layouts: 1.63 us -> none  [local(): out_shard = out_panel.T.reshape(rows, 4, -1).transpose(1, 0, 2)]
where the time goes in v4:
time: 121 us; the launch traced here: 120 us
  Pallas kernels  113 us (93%)
  local copies, waits for them, and re-layouts  6.15 us (5%)
    pallas_call x1, Pallas kernels, local(): pl.pallas_call(functools.partial(kernel, heads, seq_count), out_shape=jax...  113 us

profile of v4, /device:TPU:32, one launch (start us, length us, event | category | flops | bytes accessed | tf_op | source)
XLA Modules:
  0.0 120.1 jit_solution(11044435627801331608)
XLA Ops:
  0.7 1.7 %reshape.6 = bf16[96,2,2,8,128]{4,3,2,1,0:T(8,128)(2,1)S(1)} reshape(bf16[96,4,1024]{2,1,0:T(4,128)(2,1)} %param.6) | data formatting | bytes 1572864 | tf_op jit(solution)/shard_map/reshape | solution.py:460
  2.3 0.8 copy.8
  3.1 1.4 %reshape.7.wsh = bf16[8,2,96,256]{3,2,1,0:T(8,128)(2,1)} reshape(bf16[8,2,96,2,128]{4,3,2,1,0:T(2,128)(2,1)S(1)} %bitcast.6) | data formatting | bytes 1572864 | tf_op jit(solution)/shard_map/reshape | solution.py:461
  4.5 113.2 %shard_map.55 = bf16[768,768]{1,0:T(8,128)(2,1)} custom-call(s32[8]{0:T(128)} %powers.1, s32[1]{0:T(128)S(6)} %copy.10.place, bf16[768,3072]{1,0:T(8,128)(2,1)} %bitcast.8, bf16[8,2,96,256]{3,2,1,0:T(8,128)(2,1)} %reshape.7.wsh, bf16[96,1024]{1,0:T(8,128)(2,1)} %bitcast.9), custom_call_target="tpu_custom_call" | custom-call | flops 19327352832 | bytes 8000000 | tf_op jit(solution)/shard_map/pallas_call | solution.py:469
  117.7 2.4 %copy.11 = bf16[1,768,768]{2,1,0:T(8,128)(2,1)} copy(bf16[1,768,768]{2,1,0:T(8,128)(2,1)} %bitcast.7) | data formatting | bytes 2359296

commit v5 on v4

--- a/solution.py
+++ b/solution.py
@@ -65,10 +65,12 @@
 
     own_copies = [
         pltpu.make_async_copy(tok, tokv, loc.at[0]),
-        pltpu.make_async_copy(wsh, G.at[pl.ds(0, heads), :, y, zlo, c, zhi], loc.at[1]),
+        pltpu.make_async_copy(wsh.at[0], G.at[pl.ds(0, heads), 0, y, zlo, c, zhi], loc.at[1]),
         pltpu.make_async_copy(quarter(y), stage.at[y], loc.at[2]),
+        pltpu.make_async_copy(wsh.at[1], G.at[pl.ds(0, heads), 1, y, zlo, c, zhi], loc.at[3]),
     ]
     own_copies[1].start()
+    own_copies[3].start()
     own_copies[2].start()
     for d in (1, 2, 3):
         greet(at_y(around(y, d)))
@@ -135,7 +137,7 @@
         for a in (0, 1):
             k, at = first_ring[a]
             own = unit1(m, a, k)
-            start = wsh.at[m, a] if isinstance(m, int) else own
+            start = wsh.at[a, m] if isinstance(m, int) else own
             for d, step in ((0, 1), (1, 3)):
                 send(start, own, s1.at[k0], r1.at[k0, a, d], at(around(k, step)))
 
@@ -219,6 +221,7 @@
     own_copies[0].start()
     first_pass(0)
     own_copies[1].wait()
+    own_copies[3].wait()
     first_pass(1)
     first_end(0)
     for a in (0, 1):
@@ -457,8 +460,10 @@
     seq_count = lax.axis_size("seq")
     heads = decay_power.shape[0]
     rows = in_panels.shape[0]
-    shard = in_panels.reshape(rows, 2, 2, heads, HDIM).transpose(3, 1, 0, 2, 4)
-    shard = shard.reshape(heads, 2, rows, 2 * HDIM)
+    flat = lax.optimization_barrier(in_panels.reshape(rows, 4 * heads * HDIM))
+    tiles = flat.reshape(rows, 4 * heads, HDIM).transpose(1, 0, 2)
+    tiles = tiles.reshape(2, 2, heads, rows, HDIM)
+    shard = jnp.concatenate([tiles[:, 0], tiles[:, 1]], axis=-1)
     out_shard = out_panel.T
 
     any_space = pl.BlockSpec(memory_space=pl.ANY)
@@ -485,7 +490,7 @@
             pltpu.VMEM((heads, 4, HDIM // 4, HDIM), BF16),
             pltpu.VMEM((extent, columns), F32),
             pltpu.VMEM((4, out_panel.shape[1], out_panel.shape[0] // 4), BF16),
-            dma((3,)),
+            dma((4,)),
             dma((4,)),
             dma((4, 2, 3)),
             dma((4,)),

time: 121 us -> 121 us (level)
  local copies, waits for them, and re-layouts: 6.15 us -> 4.26 us
    reshape x3 -> x0, local copies, waits for them, and re-layouts: 3.79 us -> none  [the longest x2 2.41 us: local(): shard = in_panels.reshape(rows, 2, 2, heads, HDIM).transpose(3, 1, 0, 2, 4)]
    unnamed x1 -> x3, local copies, waits for them, and re-layouts: 2.36 us -> 3.92 us
where the time goes in v5:
time: 121 us; the launch traced here: 119 us
  Pallas kernels  113 us (93%)
  local copies, waits for them, and re-layouts  4.26 us (4%)
    pallas_call x1, Pallas kernels, local(): pl.pallas_call(functools.partial(kernel, heads, seq_count), out_shape=jax...  113 us
    unnamed x3, local copies, waits for them, and re-layouts  3.92 us

profile of v5, /device:TPU:32, one launch (start us, length us, event | category | flops | bytes accessed | tf_op | source)
XLA Modules:
  0.0 119.2 jit_solution(11133762434423343463)
XLA Ops:
  0.7 1.4 %copy.15 = bf16[12,8,4,1024]{3,1,2,0:T(8,128)(2,1)S(1)} copy(bf16[12,8,4,1024]{3,2,1,0:T(4,128)(2,1)} %bitcast.18) | data formatting | bytes 1572864
  2.1 0.2 copy.16
  2.2 0.1 fusion
  2.4 0.2 copy_bitcast_fusion
  2.6 1.0 pad_maximum_fusion.wsh
  3.6 113.3 %shard_map.55 = bf16[768,768]{1,0:T(8,128)(2,1)} custom-call(s32[8]{0:T(128)} %powers.1, s32[1]{0:T(128)S(6)} %copy.20.place, bf16[768,3072]{1,0:T(8,128)(2,1)} %bitcast.19, bf16[2,8,96,256]{3,2,1,0:T(8,128)(2,1)} %pad_maximum_fusion.wsh, bf16[96,1024]{1,0:T(8,128)(2,1)} %bitcast.20), custom_call_target="tpu_custom_call" | custom-call | flops 19327352832 | bytes 8000000 | tf_op jit(solution)/shard_map/pallas_call | solution.py:474
  116.8 2.4 %copy.21 = bf16[1,768,768]{2,1,0:T(8,128)(2,1)} copy(bf16[1,768,768]{2,1,0:T(8,128)(2,1)} %bitcast.17) | data formatting | bytes 2359296
